TPU v7x, 512 devices: a whole 4x8x8 slice. The times are simulated.
512 devices in a mesh: rows: 64 (over z, y), cols: 8 (over x, core).
Axes of the slice: x: 4, y: 8, z: 8, core: 2. Of those that a mesh axis runs over, the one named last changes fastest.
Arguments:
- grads: float32 [131072, 1024], P(('rows', 'cols')), may hold values from -6 to 6
- owners: int32 [131072, 1], P(('rows', 'cols')), may hold values from 0 to 63; in each aligned block of 256 rows (0 to 255, 256 to 511, ...) at most 8 rows name the same one
- local_ids: int32 [131072], P(('rows', 'cols')), may hold values from 0 to 1023
- params: float32 [65536, 1024], P('rows', 'cols'), may hold values from -6 to 6
- first_moment: float32 [65536, 1024], P('rows', 'cols'), may hold values from -4 to 4
- second_moment: float32 [65536, 1024], P('rows', 'cols'), may hold values from 0.0001 to 0.01
- step_count: int32 [1], replicated, may hold values from 1 to 29
Outputs:
- new_params: float32 [65536, 1024], P('rows', 'cols')
- new_first: float32 [65536, 1024], P('rows', 'cols')
- new_second: float32 [65536, 1024], P('rows', 'cols')
- row_steps: bfloat16 [131072, 1024], P(('rows', 'cols'))
Inputs may be any that keep to these rules, and one draw needn't show every extreme that they name: `owners`: among the rows of one device, at most 8 name the same owner, a bound that some block reaches of them.
All inputs are finite; a program needn't handle non-finite values.
Results may differ from a plain program's by a relative error of at most 0.001.
Values may be sent and summed in bfloat16 or wider, within the bound.
No kernel may reach another device: no remote copies, remote signals or barrier semaphores. Data moves between devices by JAX's collectives and lax.ppermute only.
A program may use at most 64 MiB of HBM per device.

v0:
```python
import jax
import jax.numpy as jnp
from jax import lax
from jax.sharding import PartitionSpec as P


def spread_out(buffers):
    return (
        lax.all_to_all(buffers[0], "cols", split_axis=2, concat_axis=1, tiled=True),
        lax.all_to_all(buffers[1], "cols", split_axis=2, concat_axis=1, tiled=True),
    )


def owners_out(buffers):
    return (
        lax.all_to_all(buffers[0], "rows", split_axis=0, concat_axis=1, tiled=True),
        lax.all_to_all(buffers[1], "rows", split_axis=0, concat_axis=1, tiled=True),
    )


def owners_back(values):
    return lax.all_to_all(values, "rows", split_axis=1, concat_axis=0, tiled=True)


def widths_back(values):
    return lax.all_to_all(values, "cols", split_axis=1, concat_axis=2, tiled=True)


def local(grads, owners, local_ids, params, first_moment, second_moment, step_count):
    groups = lax.axis_size("rows")
    slices = lax.axis_size("cols")
    grad_rows, width = grads.shape
    own_rows, slice_width = params.shape
    capacity = max(2, 2 * grad_rows // groups)
    owner_col = owners[:, 0]
    onehot = (owner_col[:, None] == jnp.arange(groups, dtype=jnp.int32)[None, :]).astype(jnp.int32)
    before = jnp.cumsum(onehot, axis=0) - onehot
    position = jnp.sum(before * onehot, axis=1)
    target = owner_col * capacity + position
    send_rows = jnp.zeros((groups * capacity, width), jnp.float32).at[target].set(grads)
    send_ids = jnp.full((groups * capacity,), own_rows, jnp.int32).at[target].set(local_ids)
    send_rows = send_rows.reshape(groups, capacity, width)
    send_ids = jnp.broadcast_to(send_ids.reshape(groups, capacity, 1), (groups, capacity, slices))
    moved = owners_out(spread_out((send_rows, send_ids)))
    got_rows = moved[0].reshape(-1, slice_width)
    got_ids = moved[1].reshape(-1)
    summed = jnp.zeros((own_rows, slice_width), jnp.float32).at[got_ids].add(got_rows, mode="drop")
    touched = jnp.zeros((own_rows,), jnp.float32).at[got_ids].add(1.0, mode="drop")
    live = (touched > 0.0)[:, None]
    new_first = jnp.where(live, 0.9 * first_moment + 0.1 * summed, first_moment)
    new_second = jnp.where(live, 0.999 * second_moment + 0.001 * summed * summed, second_moment)
    steps_done = step_count[0].astype(jnp.float32)
    fix_first = 1.0 - jnp.power(jnp.float32(0.9), steps_done)
    fix_second = 1.0 - jnp.power(jnp.float32(0.999), steps_done)
    direction = -(new_first / fix_first) / (jnp.sqrt(new_second / fix_second) + 1e-08)
    new_params = jnp.where(live, params + 0.01 * direction, params)
    direction_half = direction.astype(jnp.bfloat16)
    answer = jnp.take(direction_half, got_ids, axis=0, mode="fill", fill_value=0)
    answer = answer.reshape(1, -1, slice_width)
    returned = widths_back(owners_back(answer))
    returned = returned.reshape(groups * capacity, width)
    row_steps = returned[target]
    return (new_params, new_first, new_second, row_steps)


def solution(mesh):
    placed = (
        P(("rows", "cols"), None),
        P(("rows", "cols"), None),
        P(("rows", "cols")),
        P("rows", "cols"),
        P("rows", "cols"),
        P("rows", "cols"),
        P(),
    )
    return jax.shard_map(
        local,
        mesh=mesh,
        in_specs=placed,
        out_specs=(
            P("rows", "cols"),
            P("rows", "cols"),
            P("rows", "cols"),
            P(("rows", "cols"), None),
        ),
        check_vma=False,
    )
```

profile of v0, /device:TPU:1, one launch (start us, length us, event | category | flops | bytes accessed | tf_op | source)
XLA Modules:
  0.0 293.7 jit_solution(16779301750828560243)
XLA Ops:
  6.0 10.1 %all-to-all-start = ((s32[8,1,512]{2,1,0:T(1,128)}), s32[8,1,512]{2,1,0:T(1,128)S(1)}, u32[]{:S(2)}, u32[]{:S(2)}) async-start(s32[8,1,512]{2,1,0:T(1,128)} %reshape.196), calls=%async_computation | async-start | bytes 32768 | tf_op jit(solution)/shard_map/all_to_all | solution.py:10
  16.2 2.6 scatter_custom_fusion.2
  18.8 3.3 %copy.34 = f32[64,8,1024]{0,1,2:T(8,128)} copy(f32[64,8,1024]{2,1,0:T(8,128)S(1)} %bitcast.64) | data formatting | bytes 4194304 | tf_op jit(solution)/shard_map/reshape | solution.py:42
  22.0 7.2 %reshape.198 = f32[8,1,65536]{2,1,0:T(1,128)} reshape(f32[1024,8,64]{2,1,0:T(8,128)} %bitcast.62) | data formatting | bytes 4194304
  29.2 4.8 %all-to-all-start.2 = ((f32[8,1,65536]{2,1,0:T(1,128)}), f32[8,1,65536]{2,1,0:T(1,128)S(1)}, u32[]{:S(2)}, u32[]{:S(2)}) async-start(f32[8,1,65536]{2,1,0:T(1,128)} %reshape.198), calls=%async_computation.2 | async-start | bytes 4194304 | tf_op jit(solution)/shard_map/all_to_all | solution.py:9
  36.0 24.4 %all-to-all-done.2 = f32[8,1,65536]{2,1,0:T(1,128)S(1)} async-done(((f32[8,1,65536]{2,1,0:T(1,128)}), f32[8,1,65536]{2,1,0:T(1,128)S(1)}, u32[]{:S(2)}, u32[]{:S(2)}) %all-to-all-start.2) | async-done | bytes 2097184 | tf_op jit(solution)/shard_map/all_to_all | solution.py:9
  60.4 12.2 %all-to-all-start.1 = ((s32[64,64,1]{1,2,0:T(1,128)}), s32[64,64,1]{1,2,0:T(1,128)S(1)}, u32[]{:S(2)}, u32[]{:S(2)}) async-start(s32[64,64,1]{1,2,0:T(1,128)} %copy.33), calls=%async_computation.1 | async-start | bytes 65536 | tf_op jit(solution)/shard_map/all_to_all | solution.py:17
  73.1 7.2 %reduce.9 = f32[8,65536]{1,0:T(8,128)S(1)} reduce(f32[8,1,65536]{2,1,0:T(1,128)} %copy-done, f32[]{:T(128)} %broadcast.121), dimensions={1}, to_apply=%all_to_all.65.reduce_sub_computation | reduce | bytes 4194308 | tf_op jit(solution)/shard_map/all_to_all | solution.py:9
  80.3 3.6 %reshape.199 = f32[1024,8,64]{2,1,0:T(8,128)} reshape(f32[8,65536]{1,0:T(8,128)S(1)} %reduce.9) | data formatting | bytes 4194304
  83.9 4.5 %copy.35 = f32[64,8,8,128]{3,2,1,0:T(8,128)} copy(f32[64,8,8,128]{0,2,3,1:T(8,128)} %bitcast.63) | data formatting | bytes 4194304 | tf_op jit(solution)/shard_map/all_to_all | solution.py:9
  88.4 12.1 %all-to-all-start.3 = ((f32[64,64,128]{2,1,0:T(8,128)}), f32[64,64,128]{2,1,0:T(8,128)S(1)}, u32[]{:S(2)}, u32[]{:S(2)}) async-start(f32[64,64,128]{2,1,0:T(8,128)} %bitcast.12), calls=%async_computation.3 | async-start | bytes 4194304 | tf_op jit(solution)/shard_map/all_to_all | solution.py:16
  102.7 27.8 %scatter_custom_fusion.1 = f32[1024]{0:T(1024)S(1)} fusion(s32[4096]{0:T(1024)S(1)} %bitcast.71, f32[4096]{0:T(1024)S(1)} %broadcast.92, f32[]{:T(128)} %constant.17.clone.1), kind=kCustom, calls=%fused_computation.34 | custom fusion | flops 4096 | bytes 4100 | tf_op jit(solution)/shard_map/scatter-add | solution.py:48
  130.6 19.0 %all-to-all-done.3 = f32[64,64,128]{2,1,0:T(8,128)S(1)} async-done(((f32[64,64,128]{2,1,0:T(8,128)}), f32[64,64,128]{2,1,0:T(8,128)S(1)}, u32[]{:S(2)}, u32[]{:S(2)}) %all-to-all-start.3) | async-done | bytes 2097184 | tf_op jit(solution)/shard_map/all_to_all | solution.py:16
  149.6 22.5 %scatter_custom_fusion.3 = f32[1024,128]{1,0:T(8,128)S(1)} fusion(s32[4096]{0:T(1024)S(1)} %bitcast.73, f32[4096,128]{1,0:T(8,128)S(1)} %bitcast.69, f32[]{:T(128)} %constant.17.clone.1), kind=kCustom, calls=%fused_computation.16 | custom fusion | flops 524288 | bytes 524292 | tf_op jit(solution)/shard_map/scatter-add | solution.py:47
  172.1 2.6 fusion.14
  174.7 12.1 %gather_fusion = bf16[4096,128]{1,0:T(8,128)(2,1)S(1)} fusion(bf16[1024,128]{1,0:T(8,128)(2,1)S(1)} %get-tuple-element.4, s32[4096]{0:T(1024)S(1)} %broadcast_clamp_fusion), kind=kCustom, calls=%fused_computation | custom fusion | bytes 2113536 | tf_op jit(solution)/shard_map/jit(_take)/gather | solution.py:58
  186.8 2.1 bitcast_select_fusion
  189.0 16.7 %copy.45 = bf16[1,4096,128]{2,0,1:T(2,128)(2,1)S(1)} copy(bf16[1,4096,128]{2,1,0:T(8,128)(2,1)S(1)} %bitcast_select_fusion) | data formatting | bytes 2097152 | tf_op jit(solution)/shard_map/jit(_take)/select_n | solution.py:58
  206.3 22.4 %reduce.10 = bf16[4096,128]{1,0:T(8,128)(2,1)S(1)} reduce(bf16[4096,1,128]{2,1,0:T(2,128)(2,1)S(1)} %bitcast.66, bf16[]{:T(256)} %broadcast.122), dimensions={1}, to_apply=%bitcast.58.reduce_sub_computation | reduce | bytes 2097154
  228.9 36.8 %all_to_all.81 = bf16[64,2,4096]{2,1,0:T(2,128)(2,1)S(1)} all-to-all(bf16[64,2,4096]{2,1,0:T(2,128)(2,1)S(1)} %reshape.200), channel_id=1, replica_groups=mesh['rows'=64,'cols'=8] {'rows'}, dimensions={0} | all-to-all | bytes 2097152 | tf_op jit(solution)/shard_map/all_to_all | solution.py:22
  266.9 1.7 copy.37
  268.6 7.3 %all-to-all-start.5 = ((bf16[64,64,128]{2,0,1:T(8,128)(2,1)}), bf16[64,64,128]{2,0,1:T(8,128)(2,1)S(1)}, u32[]{:S(2)}, u32[]{:S(2)}) async-start(bf16[64,64,128]{2,0,1:T(8,128)(2,1)} %copy.37), calls=%async_computation.5 | async-start | bytes 2097152 | tf_op jit(solution)/shard_map/all_to_all | solution.py:26
  277.0 14.1 %all-to-all-done.5 = bf16[64,64,128]{2,0,1:T(8,128)(2,1)S(1)} async-done(((bf16[64,64,128]{2,0,1:T(8,128)(2,1)}), bf16[64,64,128]{2,0,1:T(8,128)(2,1)S(1)}, u32[]{:S(2)}, u32[]{:S(2)}) %all-to-all-start.5) | async-done | bytes 1048608 | tf_op jit(solution)/shard_map/all_to_all | solution.py:26
  291.7 2.0 gather_fusion.1
  (44 shorter events, 13.0 us)
Async XLA Ops:
  6.0 23.2 %all-to-all-start = ((s32[8,1,512]{2,1,0:T(1,128)}), s32[8,1,512]{2,1,0:T(1,128)S(1)}, u32[]{:S(2)}, u32[]{:S(2)}) async-start(s32[8,1,512]{2,1,0:T(1,128)} %reshape.196), calls=%async_computation | async-start | bytes 32768 | tf_op jit(solution)/shard_map/all_to_all | solution.py:10
  29.2 31.2 %all-to-all-start.2 = ((f32[8,1,65536]{2,1,0:T(1,128)}), f32[8,1,65536]{2,1,0:T(1,128)S(1)}, u32[]{:S(2)}, u32[]{:S(2)}) async-start(f32[8,1,65536]{2,1,0:T(1,128)} %reshape.198), calls=%async_computation.2 | async-start | bytes 4194304 | tf_op jit(solution)/shard_map/all_to_all | solution.py:9
  60.4 12.2 %copy-start = (f32[8,1,65536]{2,1,0:T(1,128)}, f32[8,1,65536]{2,1,0:T(1,128)S(1)}, u32[]{:S(2)}) copy-start(f32[8,1,65536]{2,1,0:T(1,128)S(1)} %all-to-all-done.2) | copy-start | bytes 6291460
  60.4 28.0 %all-to-all-start.1 = ((s32[64,64,1]{1,2,0:T(1,128)}), s32[64,64,1]{1,2,0:T(1,128)S(1)}, u32[]{:S(2)}, u32[]{:S(2)}) async-start(s32[64,64,1]{1,2,0:T(1,128)} %copy.33), calls=%async_computation.1 | async-start | bytes 65536 | tf_op jit(solution)/shard_map/all_to_all | solution.py:17
  88.4 83.6 %copy-start.2 = (f32[1024,128]{1,0:T(8,128)S(1)}, f32[1024,128]{1,0:T(8,128)}, u32[]{:S(2)}) copy-start(f32[1024,128]{1,0:T(8,128)} %param.11) | copy-start | bytes 1572868
  88.4 61.1 %all-to-all-start.3 = ((f32[64,64,128]{2,1,0:T(8,128)}), f32[64,64,128]{2,1,0:T(8,128)S(1)}, u32[]{:S(2)}, u32[]{:S(2)}) async-start(f32[64,64,128]{2,1,0:T(8,128)} %bitcast.12), calls=%async_computation.3 | async-start | bytes 4194304 | tf_op jit(solution)/shard_map/all_to_all | solution.py:16
  266.9 9.1 %copy-start.1 = (f32[1024,128]{1,0:T(8,128)S(1)}, f32[1024,128]{1,0:T(8,128)}, u32[]{:S(2)}) copy-start(f32[1024,128]{1,0:T(8,128)} %get-tuple-element.5) | copy-start | bytes 1572868
  266.9 9.0 %copy-start.3 = (f32[1024,128]{1,0:T(8,128)S(1)}, f32[1024,128]{1,0:T(8,128)}, u32[]{:S(2)}) copy-start(f32[1024,128]{1,0:T(8,128)} %param.10) | copy-start | bytes 1572868
  268.6 22.5 %all-to-all-start.5 = ((bf16[64,64,128]{2,0,1:T(8,128)(2,1)}), bf16[64,64,128]{2,0,1:T(8,128)(2,1)S(1)}, u32[]{:S(2)}, u32[]{:S(2)}) async-start(bf16[64,64,128]{2,0,1:T(8,128)(2,1)} %copy.37), calls=%async_computation.5 | async-start | bytes 2097152 | tf_op jit(solution)/shard_map/all_to_all | solution.py:26
where the time goes:
time: 295 us; the launch traced here: 294 us
  other arithmetic  90 us (31%)
  local copies, waits for them, and re-layouts  61.4 us (21%)
  waiting for transfers between devices  57.4 us (19%)
  starting transfers between devices  46.5 us (16%)
  blocking collectives  36.8 us (12%)
    all_to_all x1, blocking collectives, owners_back(): lax.all_to_all(values, 'rows', split_axis=1, concat_axis=0, tiled=True)  36.8 us
    scatter-add x1, other arithmetic, local(): jnp.zeros((own_rows,), jnp.float32).at[got_ids].add(1.0, mode='drop')  27.8 us
    all_to_all x1, waiting for transfers between devices, spread_out(): lax.all_to_all(buffers[0], 'cols', split_axis=2, concat_axis=1, tiled=True)  24.4 us
    scatter-add x1, other arithmetic, local(): jnp.zeros((own_rows, slice_width), jnp.float32).at[got_ids]  22.5 us
    unnamed x1, other arithmetic  22.4 us
    all_to_all x1, waiting for transfers between devices, owners_out(): lax.all_to_all(buffers[0], 'rows', split_axis=0, concat_axis=1, tiled=True)  19 us
    select_n x1, local copies, waits for them, and re-layouts, local(): jnp.take(direction_half, got_ids, axis=0, mode='fill', fill_value=0)  16.7 us
    all_to_all x1, waiting for transfers between devices, widths_back(): lax.all_to_all(values, 'cols', split_axis=1, concat_axis=2, tiled=True)  14.1 us
  transfers between devices with their start and end apart: 5, of which 3 were waited for; matrix products, arithmetic and copies ran while one was open for 21% of the time, Pallas kernels for 0%

commit v1 on v0

v1 whole, which is shorter than its diff:
```python
import functools

import jax
import jax.numpy as jnp
from jax import lax
from jax.experimental import pallas as pl
from jax.experimental.pallas import tpu as pltpu
from jax.sharding import PartitionSpec as P

LANES = 128
FULL = 32767.0
BIAS = 128.0
ORDER = ("cols", "rows")


def iota(shape, axis):
    return lax.broadcasted_iota(jnp.int32, shape, axis)


def dot(a, b):
    return jnp.dot(a, b, preferred_element_type=jnp.float32)


def dot_t(a, b):
    return lax.dot_general(a, b, (((0,), (0,)), ((), ())), preferred_element_type=jnp.float32)


def pack_kernel(groups, cap, owners_ref, ids_ref, grads_ref, message_ref, select_ref):
    count, width = grads_ref.shape
    words = cap // 2
    block = words + 1
    owner = owners_ref[...]
    mine = (owner == iota((count, LANES), 1)).astype(jnp.bfloat16)
    square = (count, count)
    earlier = (iota(square, 1) < iota(square, 0)).astype(jnp.bfloat16)
    before = dot(earlier, mine) * mine.astype(jnp.float32)
    position = jnp.sum(before, axis=1, keepdims=True).astype(jnp.int32)
    on_diagonal = iota(square, 0) == iota(square, 1)
    ids = jnp.sum(jnp.where(on_diagonal, ids_ref[...].astype(jnp.float32), 0.0), axis=1, keepdims=True)
    slots = iota((count, groups * cap), 1)
    select_ref[...] = (slots == owner * cap + position).astype(jnp.bfloat16)
    place = (slots == position * groups + owner).astype(jnp.bfloat16)

    grads = grads_ref[...]
    size = jnp.abs(grads)
    top = jnp.max(size, axis=1, keepdims=True)
    power = jnp.clip(jnp.ceil(jnp.log2(top)), -120.0, 100.0)
    code = jnp.minimum(jnp.floor(jnp.sqrt(size * jnp.exp2(-power)) * FULL + 0.5), FULL)
    code = jnp.where(grads < 0.0, -code, code)
    high = jnp.floor(code * (1.0 / 256.0) + 0.5)
    low = code - high * 256.0
    placed = dot_t(place, high.astype(jnp.bfloat16)) * 256.0 + dot_t(place, low.astype(jnp.bfloat16))
    placed = placed.astype(jnp.int32)

    named = ids + 1.0
    named_high = jnp.floor(named * (1.0 / 32.0))
    named_low = named - named_high * 32.0
    lane = iota((count, LANES), 1)
    facts = jnp.where(lane == position, named_high, 0.0)
    facts = facts + jnp.where(lane == position + cap, named_low, 0.0)
    facts = facts + jnp.where(lane == position + 2 * cap, power + BIAS, 0.0)
    facts = dot_t(mine, facts.astype(jnp.bfloat16))[:groups].astype(jnp.int32)

    for j in range(words):
        one = placed[j * groups : (j + 1) * groups]
        two = placed[(j + words) * groups : (j + words + 1) * groups]
        word = (one & 0xFFFF) | (two << 16)
        for c in range(width // LANES):
            rows = pl.ds(c * groups * block + j, groups, stride=block)
            message_ref[rows, :] = word[:, c * LANES : (c + 1) * LANES]
    for c in range(width // LANES):
        message_ref[pl.ds(c * groups * block + words, groups, stride=block), :] = facts


def update_kernel(
    cap, message_ref, fix_ref, params_ref, first_ref, second_ref,
    new_params_ref, new_first_ref, new_second_ref, answer_ref, spread_ref,
):
    own, lanes = params_ref.shape
    words = cap // 2
    block = words + 1
    sources = message_ref.shape[0] // block
    facts = message_ref[pl.ds(words, sources, stride=block), :].astype(jnp.float32)
    across = facts.T
    id_rows = (across[:cap] * 32.0 + across[cap : 2 * cap] - 1.0).astype(jnp.int32)
    items = iota((own, sources), 0)
    total = jnp.zeros((own, 2 * lanes), jnp.float32)
    seen = jnp.zeros((own, sources), jnp.bfloat16)
    for j in range(words):
        word = message_ref[pl.ds(j, sources, stride=block), :]
        for s, code in ((j, (word << 16) >> 16), (j + words, word >> 16)):
            scale = jnp.exp2(facts[:, 2 * cap + s : 2 * cap + s + 1] - BIAS) * (1.0 / (FULL * FULL))
            code = code.astype(jnp.float32)
            value = code * jnp.abs(code) * scale
            high = value.astype(jnp.bfloat16)
            low = (value - high.astype(jnp.float32)).astype(jnp.bfloat16)
            hit = (items == id_rows[s : s + 1]).astype(jnp.bfloat16)
            total = total + dot(hit, jnp.concatenate([high, low], axis=1))
            seen = jnp.maximum(seen, hit)
    summed = total[:, :lanes] + total[:, lanes:]
    live = jnp.max(seen.astype(jnp.float32), axis=1, keepdims=True) > 0.0
    first, second, params = first_ref[...], second_ref[...], params_ref[...]
    new_first = jnp.where(live, 0.9 * first + 0.1 * summed, first)
    new_second = jnp.where(live, 0.999 * second + 0.001 * summed * summed, second)
    direction = -(new_first / fix_ref[0]) / (jnp.sqrt(new_second / fix_ref[1]) + 1e-08)
    new_first_ref[...] = new_first
    new_second_ref[...] = new_second
    new_params_ref[...] = jnp.where(live, params + 0.01 * direction, params)

    half = own // 2
    direction = direction.astype(jnp.bfloat16)
    table = jnp.concatenate([direction[:half], direction[half:]], axis=1)
    spots = iota((sources, half), 1)
    for s in range(cap):
        id_col = (facts[:, s : s + 1] * 32.0 + facts[:, cap + s : cap + s + 1] - 1.0).astype(jnp.int32)
        upper = id_col >= half
        hit = (spots == jnp.where(upper, id_col - half, id_col)).astype(jnp.bfloat16)
        both = dot(hit, table)
        spread_ref[pl.ds(s, sources, stride=cap), :] = jnp.where(upper, both[:, lanes:], both[:, :lanes])
    answer_ref[...] = spread_ref[...].astype(jnp.bfloat16)


def unpack_kernel(select_ref, back_ref, out_ref):
    select = select_ref[...]
    slots = select.shape[1]
    for c in range(out_ref.shape[1] // LANES):
        rows = dot(select, back_ref[c * slots : (c + 1) * slots])
        out_ref[:, c * LANES : (c + 1) * LANES] = rows.astype(jnp.bfloat16)


VMEM = pl.BlockSpec(memory_space=pltpu.VMEM)
SMEM = pl.BlockSpec(memory_space=pltpu.SMEM)


def params_for(mib):
    return pltpu.CompilerParams(vmem_limit_bytes=mib * 1024 * 1024)


def local(grads, owners, local_ids, params, first_moment, second_moment, step_count):
    groups = lax.axis_size("rows")
    slices = lax.axis_size("cols")
    count, width = grads.shape
    own, lanes = params.shape
    cap = max(2, 2 * count // groups)
    block = cap // 2 + 1
    peers = groups * slices
    message, select = pl.pallas_call(
        functools.partial(pack_kernel, groups, cap),
        out_shape=(
            jax.ShapeDtypeStruct((peers * block, lanes), jnp.int32),
            jax.ShapeDtypeStruct((count, groups * cap), jnp.bfloat16),
        ),
        in_specs=[VMEM, VMEM, VMEM],
        out_specs=(VMEM, VMEM),
        compiler_params=params_for(40),
        name="pack",
    )(owners, local_ids.reshape(1, count), grads)
    message = message.reshape(peers, 1, block * lanes)
    message = lax.all_to_all(message, ORDER, split_axis=0, concat_axis=0, tiled=True)
    message = message.reshape(peers * block, lanes)
    steps_done = step_count[0].astype(jnp.float32)
    fix_first = 1.0 - jnp.power(jnp.float32(0.9), steps_done)
    fix_second = 1.0 - jnp.power(jnp.float32(0.999), steps_done)
    table = jax.ShapeDtypeStruct((own, lanes), jnp.float32)
    new_params, new_first, new_second, answer = pl.pallas_call(
        functools.partial(update_kernel, cap),
        out_shape=(table, table, table, jax.ShapeDtypeStruct((peers * cap, lanes), jnp.bfloat16)),
        in_specs=[VMEM, SMEM, VMEM, VMEM, VMEM],
        out_specs=(VMEM, VMEM, VMEM, VMEM),
        scratch_shapes=[pltpu.VMEM((peers * cap, lanes), jnp.float32)],
        compiler_params=params_for(48),
        name="update",
    )(message, jnp.stack([fix_first, fix_second]), params, first_moment, second_moment)
    answer = answer.reshape(peers, cap, lanes)
    answer = lax.all_to_all(answer, ORDER, split_axis=0, concat_axis=0, tiled=True)
    row_steps = pl.pallas_call(
        unpack_kernel,
        out_shape=jax.ShapeDtypeStruct((count, width), jnp.bfloat16),
        in_specs=[VMEM, VMEM],
        out_specs=VMEM,
        compiler_params=params_for(40),
        name="unpack",
    )(select, answer.reshape(peers * cap, lanes))
    return (new_params, new_first, new_second, row_steps)


def solution(mesh):
    placed = (
        P(("rows", "cols"), None),
        P(("rows", "cols"), None),
        P(("rows", "cols")),
        P("rows", "cols"),
        P("rows", "cols"),
        P("rows", "cols"),
        P(),
    )
    return jax.shard_map(
        local,
        mesh=mesh,
        in_specs=placed,
        out_specs=(
            P("rows", "cols"),
            P("rows", "cols"),
            P("rows", "cols"),
            P(("rows", "cols"), None),
        ),
        check_vma=False,
    )
```

time: 295 us -> 122 us (0.41)
  other arithmetic: 90 us -> 0.08 us
  local copies, waits for them, and re-layouts: 61.4 us -> 2.72 us
  starting transfers between devices: 46.5 us -> 22.2 us
  waiting for transfers between devices: 57.4 us -> 38.5 us
  Pallas kernels: 0 us -> 13.6 us
  blocking collectives: 36.8 us -> 43 us
    scatter-add x2 -> x0, other arithmetic: 50.3 us -> none  [the longest x1 27.8 us: local(): jnp.zeros((own_rows,), jnp.float32).at[got_ids].add(1.0, mode='drop')]
    all_to_all x5 -> x1, starting transfers between devices: 46.5 us -> 22.2 us  [local(): lax.all_to_all(message, ORDER, split_axis=0, concat_axis=0, tiled=True)]
    unnamed x1 -> x0, other arithmetic: 22.4 us -> none
    all_to_all x5 -> x1, waiting for transfers between devices: 57.4 us -> 38.5 us  [local(): lax.all_to_all(message, ORDER, split_axis=0, concat_axis=0, tiled=True)]
    select_n x1 -> x0, local copies, waits for them, and re-layouts: 16.7 us -> none  [local(): jnp.take(direction_half, got_ids, axis=0, mode='fill', fill_value=0)]
    gather x2 -> x0, local copies, waits for them, and re-layouts: 14.1 us -> none  [the longest x1 12.1 us: local(): jnp.take(direction_half, got_ids, axis=0, mode='fill', fill_value=0)]
    pallas_call x0 -> x3, Pallas kernels: none -> 13.6 us  [the longest x1 9.26 us: local(): pl.pallas_call(functools.partial(update_kernel, cap), out_shape=(table, t...]
    unnamed x17 -> x11, local copies, waits for them, and re-layouts: 13.6 us -> 2.72 us
  transfers between devices with their start and end apart: 5 -> 1, of which waited for: 3 -> 1; matrix products, arithmetic and copies ran while one was open for 21% -> 0% of each run, Pallas kernels for 0% -> 0%
where the time goes in v1:
time: 122 us
  blocking collectives  43 us (35%)
  waiting for transfers between devices  38.5 us (32%)
  starting transfers between devices  22.2 us (18%)
  Pallas kernels  13.6 us (11%)
  local copies, waits for them, and re-layouts  2.72 us (2%)
  between operations  1.4 us (1%)
    all_to_all x1, blocking collectives, local(): lax.all_to_all(answer, ORDER, split_axis=0, concat_axis=0, tiled=True)  43 us
    all_to_all x1, waiting for transfers between devices, local(): lax.all_to_all(message, ORDER, split_axis=0, concat_axis=0, tiled=True)  38.5 us
    all_to_all x1, starting transfers between devices, local(): lax.all_to_all(message, ORDER, split_axis=0, concat_axis=0, tiled=True)  22.2 us
    pallas_call x1, Pallas kernels, local(): pl.pallas_call(functools.partial(update_kernel, cap), out_shape=(table, t...  9.26 us
    pallas_call x1, Pallas kernels, local(): pl.pallas_call(functools.partial(pack_kernel, groups, cap), out_shape=(ja...  2.85 us
    unnamed x11, local copies, waits for them, and re-layouts  2.72 us
  transfers between devices with their start and end apart: 1, of which 1 were waited for; matrix products, arithmetic and copies ran while one was open for 0% of the time, Pallas kernels for 0%

profile of v1, /device:TPU:1, one launch (start us, length us, event | category | flops | bytes accessed | tf_op | source)
XLA Modules:
  0.0 121.5 jit_solution(17842052674909122176)
XLA Ops:
  0.6 0.8 copy.12.owners_ref
  1.4 0.0 copy-start
  1.5 1.2 %copy-done = f32[256,1024]{1,0:T(8,128)S(1)} copy-done((f32[256,1024]{1,0:T(8,128)S(1)}, f32[256,1024]{1,0:T(8,128)}, u32[]{:S(2)}) %copy-start) | copy-done | bytes 1048600
  2.7 0.0 copy-start.4
  2.7 0.7 copy-done.4
  3.4 2.9 %pack.1 = (s32[2560,128]{1,0:T(8,128)}, bf16[256,512]{1,0:T(8,128)(2,1)S(1)}) custom-call(s32[256,1]{1,0:T(8,128)S(1)} %copy.12.owners_ref, s32[1,256]{1,0:T(1,128)S(1)} %bitcast.8, f32[256,1024]{1,0:T(8,128)S(1)} %copy-done), custom_call_target="tpu_custom_call" | custom-call | tf_op jit(solution)/shard_map/pack/pallas_call | solution.py:147
  6.2 0.0 copy-start.1
  6.2 0.0 copy-start.2
  6.2 0.0 copy-start.3
  6.2 22.2 %all-to-all-start = ((s32[512,1,640]{2,1,0:T(1,128)}), s32[512,1,640]{2,1,0:T(1,128)S(1)}, u32[]{:S(2)}, u32[]{:S(2)}) async-start(s32[512,1,640]{2,1,0:T(1,128)} %bitcast.1), calls=%async_computation | async-start | bytes 2621440 | tf_op jit(solution)/shard_map/all_to_all | solution.py:159
  29.1 0.1 pad_maximum_fusion.fix_ref
  29.2 38.5 %all-to-all-done = s32[512,1,640]{2,1,0:T(1,128)S(1)} async-done(((s32[512,1,640]{2,1,0:T(1,128)}), s32[512,1,640]{2,1,0:T(1,128)S(1)}, u32[]{:S(2)}, u32[]{:S(2)}) %all-to-all-start) | async-done | bytes 1310752 | tf_op jit(solution)/shard_map/all_to_all | solution.py:159
  67.7 0.0 copy-done.1
  67.7 0.0 copy-done.2
  67.7 0.0 copy-done.3
  67.7 9.3 %update.1 = (f32[1024,128]{1,0:T(8,128)}, f32[1024,128]{1,0:T(8,128)}, f32[1024,128]{1,0:T(8,128)}, bf16[4096,128]{1,0:T(8,128)(2,1)S(1)}) custom-call(s32[2560,128]{1,0:T(8,128)S(1)} %bitcast.5, f32[2]{0:T(128)S(1)} %pad_maximum_fusion.fix_ref, f32[1024,128]{1,0:T(8,128)S(1)} %copy-done.1, f32[1024,128]{1,0:T(8,128)S(1)} %copy-done.2, f32[1024,128]{1,0:T(8,128)S(1)} %copy-done.3), custom_call_target="tpu_custom_call" | custom-call | tf_op jit(solution)/shard_map/update/pallas_call | solution.py:165
  77.0 43.0 %all_to_all.10 = bf16[512,8,128]{2,1,0:T(8,128)(2,1)S(1)} all-to-all(bf16[512,8,128]{2,1,0:T(8,128)(2,1)S(1)} %bitcast.7), channel_id=1, replica_groups=mesh['rows'=64,'cols'=8] {'cols','rows'}, dimensions={0} | all-to-all | bytes 2097152 | tf_op jit(solution)/shard_map/all_to_all | solution.py:175
  120.0 1.5 %unpack.1 = bf16[256,1024]{1,0:T(8,128)(2,1)} custom-call(bf16[256,512]{1,0:T(8,128)(2,1)S(1)} %get-tuple-element.14.select_ref, bf16[4096,128]{1,0:T(8,128)(2,1)S(1)} %bitcast.6), custom_call_target="tpu_custom_call" | custom-call | tf_op jit(solution)/shard_map/unpack/pallas_call | solution.py:176
Async XLA Ops:
  1.4 1.2 %copy-start = (f32[256,1024]{1,0:T(8,128)S(1)}, f32[256,1024]{1,0:T(8,128)}, u32[]{:S(2)}) copy-start(f32[256,1024]{1,0:T(8,128)} %grads_ref.1) | copy-start | bytes 3145732
  2.7 0.7 copy-start.4
  6.2 61.5 %copy-start.1 = (f32[1024,128]{1,0:T(8,128)S(1)}, f32[1024,128]{1,0:T(8,128)}, u32[]{:S(2)}) copy-start(f32[1024,128]{1,0:T(8,128)} %params_ref.1) | copy-start | bytes 1572868
  6.2 61.5 %copy-start.2 = (f32[1024,128]{1,0:T(8,128)S(1)}, f32[1024,128]{1,0:T(8,128)}, u32[]{:S(2)}) copy-start(f32[1024,128]{1,0:T(8,128)} %first_ref.1) | copy-start | bytes 1572868
  6.2 61.5 %copy-start.3 = (f32[1024,128]{1,0:T(8,128)S(1)}, f32[1024,128]{1,0:T(8,128)}, u32[]{:S(2)}) copy-start(f32[1024,128]{1,0:T(8,128)} %second_ref.1) | copy-start | bytes 1572868
  6.2 61.5 %all-to-all-start = ((s32[512,1,640]{2,1,0:T(1,128)}), s32[512,1,640]{2,1,0:T(1,128)S(1)}, u32[]{:S(2)}, u32[]{:S(2)}) async-start(s32[512,1,640]{2,1,0:T(1,128)} %bitcast.1), calls=%async_computation | async-start | bytes 2621440 | tf_op jit(solution)/shard_map/all_to_all | solution.py:159

commit v2 on v1

--- a/solution.py
+++ b/solution.py
@@ -9,7 +9,6 @@
 
 LANES = 128
 FULL = 32767.0
-BIAS = 128.0
 ORDER = ("cols", "rows")
 
 
@@ -25,18 +24,20 @@
     return lax.dot_general(a, b, (((0,), (0,)), ((), ())), preferred_element_type=jnp.float32)
 
 
-def pack_kernel(groups, cap, owners_ref, ids_ref, grads_ref, message_ref, select_ref):
+def pack_kernel(groups, cap, own, items_ref, grads_ref, message_ref, select_ref):
     count, width = grads_ref.shape
     words = cap // 2
     block = words + 1
-    owner = owners_ref[...]
+    square = (count, count)
+    on_diagonal = iota(square, 0) == iota(square, 1)
+    item = items_ref[0:1] * own + items_ref[1:2]
+    item = jnp.sum(jnp.where(on_diagonal, item.astype(jnp.float32), 0.0), axis=1, keepdims=True)
+    item = item.astype(jnp.int32)
+    owner = lax.div(item, own)
     mine = (owner == iota((count, LANES), 1)).astype(jnp.bfloat16)
-    square = (count, count)
     earlier = (iota(square, 1) < iota(square, 0)).astype(jnp.bfloat16)
     before = dot(earlier, mine) * mine.astype(jnp.float32)
     position = jnp.sum(before, axis=1, keepdims=True).astype(jnp.int32)
-    on_diagonal = iota(square, 0) == iota(square, 1)
-    ids = jnp.sum(jnp.where(on_diagonal, ids_ref[...].astype(jnp.float32), 0.0), axis=1, keepdims=True)
     slots = iota((count, groups * cap), 1)
     select_ref[...] = (slots == owner * cap + position).astype(jnp.bfloat16)
     place = (slots == position * groups + owner).astype(jnp.bfloat16)
@@ -49,18 +50,18 @@
     code = jnp.where(grads < 0.0, -code, code)
     high = jnp.floor(code * (1.0 / 256.0) + 0.5)
     low = code - high * 256.0
+
+    named = lax.rem(item, own) + 1
+    lane = iota((count, LANES), 1)
+    at_id = lane == position
+    at_power = lane == position + cap
+    facts_high = jnp.where(at_id, lax.div(named, 32).astype(jnp.float32), 0.0)
+    facts_low = jnp.where(at_id, lax.rem(named, 32).astype(jnp.float32), jnp.where(at_power, power, 0.0))
+    facts = dot_t(mine, facts_high.astype(jnp.bfloat16)) * 32.0 + dot_t(mine, facts_low.astype(jnp.bfloat16))
+    facts = facts[:groups].astype(jnp.int32)
+
     placed = dot_t(place, high.astype(jnp.bfloat16)) * 256.0 + dot_t(place, low.astype(jnp.bfloat16))
     placed = placed.astype(jnp.int32)
-
-    named = ids + 1.0
-    named_high = jnp.floor(named * (1.0 / 32.0))
-    named_low = named - named_high * 32.0
-    lane = iota((count, LANES), 1)
-    facts = jnp.where(lane == position, named_high, 0.0)
-    facts = facts + jnp.where(lane == position + cap, named_low, 0.0)
-    facts = facts + jnp.where(lane == position + 2 * cap, power + BIAS, 0.0)
-    facts = dot_t(mine, facts.astype(jnp.bfloat16))[:groups].astype(jnp.int32)
-
     for j in range(words):
         one = placed[j * groups : (j + 1) * groups]
         two = placed[(j + words) * groups : (j + words + 1) * groups]
@@ -74,50 +75,70 @@
 
 def update_kernel(
     cap, message_ref, fix_ref, params_ref, first_ref, second_ref,
-    new_params_ref, new_first_ref, new_second_ref, answer_ref, spread_ref,
+    new_params_hbm, new_first_hbm, new_second_hbm, answer_ref, spread_ref, table_ref, table_sem,
 ):
     own, lanes = params_ref.shape
     words = cap // 2
     block = words + 1
     sources = message_ref.shape[0] // block
-    facts = message_ref[pl.ds(words, sources, stride=block), :].astype(jnp.float32)
-    across = facts.T
-    id_rows = (across[:cap] * 32.0 + across[cap : 2 * cap] - 1.0).astype(jnp.int32)
-    items = iota((own, sources), 0)
+    facts = message_ref[pl.ds(words, sources, stride=block), :]
+    across = facts.astype(jnp.float32).T
+    id_rows = across[:cap].astype(jnp.int32) - 1
+    scale_rows = jnp.exp2(across[cap : 2 * cap]).astype(jnp.bfloat16)
+    short_rows = id_rows.astype(jnp.int16)
+    items = iota((own, sources), 0).astype(jnp.int16)
     total = jnp.zeros((own, 2 * lanes), jnp.float32)
-    seen = jnp.zeros((own, sources), jnp.bfloat16)
     for j in range(words):
         word = message_ref[pl.ds(j, sources, stride=block), :]
         for s, code in ((j, (word << 16) >> 16), (j + words, word >> 16)):
-            scale = jnp.exp2(facts[:, 2 * cap + s : 2 * cap + s + 1] - BIAS) * (1.0 / (FULL * FULL))
             code = code.astype(jnp.float32)
-            value = code * jnp.abs(code) * scale
+            value = code * jnp.abs(code)
             high = value.astype(jnp.bfloat16)
             low = (value - high.astype(jnp.float32)).astype(jnp.bfloat16)
-            hit = (items == id_rows[s : s + 1]).astype(jnp.bfloat16)
+            hit = jnp.where(items == short_rows[s : s + 1], scale_rows[s : s + 1], jnp.bfloat16(0))
             total = total + dot(hit, jnp.concatenate([high, low], axis=1))
-            seen = jnp.maximum(seen, hit)
-    summed = total[:, :lanes] + total[:, lanes:]
-    live = jnp.max(seen.astype(jnp.float32), axis=1, keepdims=True) > 0.0
+    fine = 32
+    coarse = own // fine
+    counts = jnp.zeros((coarse, fine), jnp.float32)
+    for s in range(cap):
+        row = id_rows[s : s + 1]
+        whole = (iota((coarse, sources), 0) == lax.div(row, fine)).astype(jnp.bfloat16)
+        rest = (iota((fine, sources), 0) == lax.rem(row, fine)).astype(jnp.bfloat16)
+        counts = counts + lax.dot_general(whole, rest, (((1,), (1,)), ((), ())), preferred_element_type=jnp.float32)
+    counts = jnp.minimum(counts, 1.0).astype(jnp.bfloat16)
+    whole = (lax.div(iota((own, coarse), 0), fine) == iota((own, coarse), 1)).astype(jnp.bfloat16)
+    rest = lax.rem(iota((own, fine), 0), fine) == iota((own, fine), 1)
+    live = jnp.sum(jnp.where(rest, dot(whole, counts), 0.0), axis=1, keepdims=True) > 0.0
+    summed = (total[:, :lanes] + total[:, lanes:]) * (1.0 / (FULL * FULL))
     first, second, params = first_ref[...], second_ref[...], params_ref[...]
     new_first = jnp.where(live, 0.9 * first + 0.1 * summed, first)
     new_second = jnp.where(live, 0.999 * second + 0.001 * summed * summed, second)
     direction = -(new_first / fix_ref[0]) / (jnp.sqrt(new_second / fix_ref[1]) + 1e-08)
-    new_first_ref[...] = new_first
-    new_second_ref[...] = new_second
-    new_params_ref[...] = jnp.where(live, params + 0.01 * direction, params)
+    table_ref[0] = jnp.where(live, params + 0.01 * direction, params)
+    table_ref[1] = new_first
+    table_ref[2] = new_second
+    copies = [
+        pltpu.make_async_copy(table_ref.at[n], out, table_sem.at[n])
+        for n, out in enumerate((new_params_hbm, new_first_hbm, new_second_hbm))
+    ]
+    for copy in copies:
+        copy.start()
 
     half = own // 2
     direction = direction.astype(jnp.bfloat16)
     table = jnp.concatenate([direction[:half], direction[half:]], axis=1)
-    spots = iota((sources, half), 1)
+    spots = iota((sources, half), 1).astype(jnp.int16)
+    ids = facts - 1
     for s in range(cap):
-        id_col = (facts[:, s : s + 1] * 32.0 + facts[:, cap + s : cap + s + 1] - 1.0).astype(jnp.int32)
-        upper = id_col >= half
-        hit = (spots == jnp.where(upper, id_col - half, id_col)).astype(jnp.bfloat16)
+        wanted = jnp.broadcast_to(ids[:, s : s + 1], (sources, lanes))
+        upper = wanted >= half
+        spot = jnp.where(upper, wanted - half, wanted).astype(jnp.int16)
+        hit = (spots == jnp.concatenate([spot] * (half // lanes), axis=1)).astype(jnp.bfloat16)
         both = dot(hit, table)
         spread_ref[pl.ds(s, sources, stride=cap), :] = jnp.where(upper, both[:, lanes:], both[:, :lanes])
     answer_ref[...] = spread_ref[...].astype(jnp.bfloat16)
+    for copy in copies:
+        copy.wait()
 
 
 def unpack_kernel(select_ref, back_ref, out_ref):
@@ -129,6 +150,7 @@
 
 
 VMEM = pl.BlockSpec(memory_space=pltpu.VMEM)
+HBM = pl.BlockSpec(memory_space=pltpu.HBM)
 SMEM = pl.BlockSpec(memory_space=pltpu.SMEM)
 
 
@@ -144,17 +166,18 @@
     cap = max(2, 2 * count // groups)
     block = cap // 2 + 1
     peers = groups * slices
+    items = jnp.concatenate([owners.reshape(1, count), local_ids.reshape(1, count)], axis=0)
     message, select = pl.pallas_call(
-        functools.partial(pack_kernel, groups, cap),
+        functools.partial(pack_kernel, groups, cap, own),
         out_shape=(
             jax.ShapeDtypeStruct((peers * block, lanes), jnp.int32),
             jax.ShapeDtypeStruct((count, groups * cap), jnp.bfloat16),
         ),
-        in_specs=[VMEM, VMEM, VMEM],
+        in_specs=[VMEM, VMEM],
         out_specs=(VMEM, VMEM),
         compiler_params=params_for(40),
         name="pack",
-    )(owners, local_ids.reshape(1, count), grads)
+    )(items, grads)
     message = message.reshape(peers, 1, block * lanes)
     message = lax.all_to_all(message, ORDER, split_axis=0, concat_axis=0, tiled=True)
     message = message.reshape(peers * block, lanes)
@@ -166,8 +189,12 @@
         functools.partial(update_kernel, cap),
         out_shape=(table, table, table, jax.ShapeDtypeStruct((peers * cap, lanes), jnp.bfloat16)),
         in_specs=[VMEM, SMEM, VMEM, VMEM, VMEM],
-        out_specs=(VMEM, VMEM, VMEM, VMEM),
-        scratch_shapes=[pltpu.VMEM((peers * cap, lanes), jnp.float32)],
+        out_specs=(HBM, HBM, HBM, VMEM),
+        scratch_shapes=[
+            pltpu.VMEM((peers * cap, lanes), jnp.float32),
+            pltpu.VMEM((3, own, lanes), jnp.float32),
+            pltpu.SemaphoreType.DMA((3,)),
+        ],
         compiler_params=params_for(48),
         name="update",
     )(message, jnp.stack([fix_first, fix_second]), params, first_moment, second_moment)

time: 122 us -> 119 us (0.975)
  Pallas kernels: 13.6 us -> 11.3 us
  local copies, waits for them, and re-layouts: 2.72 us -> 1.24 us
    pallas_call x1, Pallas kernels: 9.26 us -> 6.77 us  [local(): pl.pallas_call(functools.partial(update_kernel, cap), out_shape=(table, t...]
    unnamed x11 -> x8, local copies, waits for them, and re-layouts: 2.72 us -> 1.24 us
where the time goes in v2:
time: 119 us
  blocking collectives  43.2 us (36%)
  waiting for transfers between devices  38.5 us (32%)
  starting transfers between devices  22.2 us (19%)
  Pallas kernels  11.3 us (9%)
  between operations  1.39 us (1%)
  local copies, waits for them, and re-layouts  1.24 us (1%)
    all_to_all x1, blocking collectives, local(): lax.all_to_all(answer, ORDER, split_axis=0, concat_axis=0, tiled=True)  43.2 us
    all_to_all x1, waiting for transfers between devices, local(): lax.all_to_all(message, ORDER, split_axis=0, concat_axis=0, tiled=True)  38.5 us
    all_to_all x1, starting transfers between devices, local(): lax.all_to_all(message, ORDER, split_axis=0, concat_axis=0, tiled=True)  22.2 us
    pallas_call x1, Pallas kernels, local(): pl.pallas_call(functools.partial(update_kernel, cap), out_shape=(table, t...  6.77 us
    pallas_call x1, Pallas kernels, local(): pl.pallas_call(functools.partial(pack_kernel, groups, cap, own), out_shap...  3.02 us
  transfers between devices with their start and end apart: 1, of which 1 were waited for; matrix products, arithmetic and copies ran while one was open for 0% of the time, Pallas kernels for 0%

profile of v2, /device:TPU:1, one launch (start us, length us, event | category | flops | bytes accessed | tf_op | source)
XLA Modules:
  0.0 118.6 jit_solution(4700223431260171302)
XLA Ops:
  0.6 0.7 pad_add_fusion.items_ref
  1.3 0.0 copy-start
  1.3 1.2 %copy-done = f32[256,1024]{1,0:T(8,128)S(1)} copy-done((f32[256,1024]{1,0:T(8,128)S(1)}, f32[256,1024]{1,0:T(8,128)}, u32[]{:S(2)}) %copy-start) | copy-done | bytes 1048600
  2.6 3.0 %pack.1 = (s32[2560,128]{1,0:T(8,128)}, bf16[256,512]{1,0:T(8,128)(2,1)S(1)}) custom-call(s32[2,256]{1,0:T(2,128)S(1)} %pad_add_fusion.items_ref, f32[256,1024]{1,0:T(8,128)S(1)} %copy-done), custom_call_target="tpu_custom_call" | custom-call | tf_op jit(solution)/shard_map/pack/pallas_call | solution.py:170
  5.6 0.0 copy-start.1
  5.6 0.0 copy-start.2
  5.6 0.0 copy-start.3
  5.6 22.2 %all-to-all-start = ((s32[512,1,640]{2,1,0:T(1,128)}), s32[512,1,640]{2,1,0:T(1,128)S(1)}, u32[]{:S(2)}, u32[]{:S(2)}) async-start(s32[512,1,640]{2,1,0:T(1,128)} %bitcast.2), calls=%async_computation | async-start | bytes 2621440 | tf_op jit(solution)/shard_map/all_to_all | solution.py:182
  28.5 0.1 pad_maximum_fusion.fix_ref
  28.6 38.5 %all-to-all-done = s32[512,1,640]{2,1,0:T(1,128)S(1)} async-done(((s32[512,1,640]{2,1,0:T(1,128)}), s32[512,1,640]{2,1,0:T(1,128)S(1)}, u32[]{:S(2)}, u32[]{:S(2)}) %all-to-all-start) | async-done | bytes 1310752 | tf_op jit(solution)/shard_map/all_to_all | solution.py:182
  67.1 0.0 copy-done.1
  67.1 0.0 copy-done.2
  67.1 0.0 copy-done.3
  67.1 6.8 %update.1 = (f32[1024,128]{1,0:T(8,128)}, f32[1024,128]{1,0:T(8,128)}, f32[1024,128]{1,0:T(8,128)}, bf16[4096,128]{1,0:T(8,128)(2,1)S(1)}) custom-call(s32[2560,128]{1,0:T(8,128)S(1)} %bitcast.6, f32[2]{0:T(128)S(1)} %pad_maximum_fusion.fix_ref, f32[1024,128]{1,0:T(8,128)S(1)} %copy-done.1, f32[1024,128]{1,0:T(8,128)S(1)} %copy-done.2, f32[1024,128]{1,0:T(8,128)S(1)} %copy-done.3), custom_call_target="tpu_custom_call" | custom-call | tf_op jit(solution)/shard_map/update/pallas_call | solution.py:188
  73.9 43.2 %all_to_all.10 = bf16[512,8,128]{2,1,0:T(8,128)(2,1)S(1)} all-to-all(bf16[512,8,128]{2,1,0:T(8,128)(2,1)S(1)} %bitcast.8), channel_id=1, replica_groups=mesh['rows'=64,'cols'=8] {'cols','rows'}, dimensions={0} | all-to-all | bytes 2097152 | tf_op jit(solution)/shard_map/all_to_all | solution.py:202
  117.1 1.5 %unpack.1 = bf16[256,1024]{1,0:T(8,128)(2,1)} custom-call(bf16[256,512]{1,0:T(8,128)(2,1)S(1)} %get-tuple-element.14.select_ref, bf16[4096,128]{1,0:T(8,128)(2,1)S(1)} %bitcast.7), custom_call_target="tpu_custom_call" | custom-call | tf_op jit(solution)/shard_map/unpack/pallas_call | solution.py:203
Async XLA Ops:
  1.3 1.2 %copy-start = (f32[256,1024]{1,0:T(8,128)S(1)}, f32[256,1024]{1,0:T(8,128)}, u32[]{:S(2)}) copy-start(f32[256,1024]{1,0:T(8,128)} %grads_ref.1) | copy-start | bytes 3145732
  5.6 61.5 %copy-start.1 = (f32[1024,128]{1,0:T(8,128)S(1)}, f32[1024,128]{1,0:T(8,128)}, u32[]{:S(2)}) copy-start(f32[1024,128]{1,0:T(8,128)} %params_ref.1) | copy-start | bytes 1572868
  5.6 61.5 %copy-start.2 = (f32[1024,128]{1,0:T(8,128)S(1)}, f32[1024,128]{1,0:T(8,128)}, u32[]{:S(2)}) copy-start(f32[1024,128]{1,0:T(8,128)} %first_ref.1) | copy-start | bytes 1572868
  5.6 61.5 %copy-start.3 = (f32[1024,128]{1,0:T(8,128)S(1)}, f32[1024,128]{1,0:T(8,128)}, u32[]{:S(2)}) copy-start(f32[1024,128]{1,0:T(8,128)} %second_ref.1) | copy-start | bytes 1572868
  5.6 61.5 %all-to-all-start = ((s32[512,1,640]{2,1,0:T(1,128)}), s32[512,1,640]{2,1,0:T(1,128)S(1)}, u32[]{:S(2)}, u32[]{:S(2)}) async-start(s32[512,1,640]{2,1,0:T(1,128)} %bitcast.2), calls=%async_computation | async-start | bytes 2621440 | tf_op jit(solution)/shard_map/all_to_all | solution.py:182

commit v3 on v2

--- a/solution.py
+++ b/solution.py
@@ -20,27 +20,25 @@
     return jnp.dot(a, b, preferred_element_type=jnp.float32)
 
 
-def dot_t(a, b):
-    return lax.dot_general(a, b, (((0,), (0,)), ((), ())), preferred_element_type=jnp.float32)
-
-
-def pack_kernel(groups, cap, own, items_ref, grads_ref, message_ref, select_ref):
+def dot_nt(a, b):
+    return lax.dot_general(a, b, (((1,), (1,)), ((), ())), preferred_element_type=jnp.float32)
+
+
+def pack_kernel(groups, cap, own, names_ref, grads_ref, message_ref, select_ref):
     count, width = grads_ref.shape
     words = cap // 2
     block = words + 1
+    slices = width // LANES
+    share = groups * block
+    owner = names_ref[0:1]
+    mine = owner == iota((groups, count), 0)
+    mine_half = mine.astype(jnp.bfloat16)
     square = (count, count)
+    earlier = (iota(square, 0) < iota(square, 1)).astype(jnp.bfloat16)
+    before = jnp.where(mine, dot(mine_half, earlier), 0.0)
+    position = jnp.sum(before, axis=0, keepdims=True).astype(jnp.int32)
+    place = (iota((groups * cap, count), 0) == position * groups + owner).astype(jnp.bfloat16)
     on_diagonal = iota(square, 0) == iota(square, 1)
-    item = items_ref[0:1] * own + items_ref[1:2]
-    item = jnp.sum(jnp.where(on_diagonal, item.astype(jnp.float32), 0.0), axis=1, keepdims=True)
-    item = item.astype(jnp.int32)
-    owner = lax.div(item, own)
-    mine = (owner == iota((count, LANES), 1)).astype(jnp.bfloat16)
-    earlier = (iota(square, 1) < iota(square, 0)).astype(jnp.bfloat16)
-    before = dot(earlier, mine) * mine.astype(jnp.float32)
-    position = jnp.sum(before, axis=1, keepdims=True).astype(jnp.int32)
-    slots = iota((count, groups * cap), 1)
-    select_ref[...] = (slots == owner * cap + position).astype(jnp.bfloat16)
-    place = (slots == position * groups + owner).astype(jnp.bfloat16)
 
     grads = grads_ref[...]
     size = jnp.abs(grads)
@@ -49,28 +47,32 @@
     code = jnp.minimum(jnp.floor(jnp.sqrt(size * jnp.exp2(-power)) * FULL + 0.5), FULL)
     code = jnp.where(grads < 0.0, -code, code)
     high = jnp.floor(code * (1.0 / 256.0) + 0.5)
-    low = code - high * 256.0
-
-    named = lax.rem(item, own) + 1
-    lane = iota((count, LANES), 1)
+    low = (code - high * 256.0).astype(jnp.bfloat16)
+    high = high.astype(jnp.bfloat16)
+
+    power_row = jnp.sum(jnp.where(on_diagonal, power, 0.0), axis=0, keepdims=True)
+    named = names_ref[1:2] + 1
+    lane = iota((LANES, count), 0)
     at_id = lane == position
     at_power = lane == position + cap
-    facts_high = jnp.where(at_id, lax.div(named, 32).astype(jnp.float32), 0.0)
-    facts_low = jnp.where(at_id, lax.rem(named, 32).astype(jnp.float32), jnp.where(at_power, power, 0.0))
-    facts = dot_t(mine, facts_high.astype(jnp.bfloat16)) * 32.0 + dot_t(mine, facts_low.astype(jnp.bfloat16))
-    facts = facts[:groups].astype(jnp.int32)
-
-    placed = dot_t(place, high.astype(jnp.bfloat16)) * 256.0 + dot_t(place, low.astype(jnp.bfloat16))
-    placed = placed.astype(jnp.int32)
-    for j in range(words):
-        one = placed[j * groups : (j + 1) * groups]
-        two = placed[(j + words) * groups : (j + words + 1) * groups]
-        word = (one & 0xFFFF) | (two << 16)
-        for c in range(width // LANES):
-            rows = pl.ds(c * groups * block + j, groups, stride=block)
-            message_ref[rows, :] = word[:, c * LANES : (c + 1) * LANES]
-    for c in range(width // LANES):
-        message_ref[pl.ds(c * groups * block + words, groups, stride=block), :] = facts
+    facts_high = jnp.where(at_id, lax.div(named, 32).astype(jnp.float32), 0.0).astype(jnp.bfloat16)
+    facts_low = jnp.where(at_id, lax.rem(named, 32).astype(jnp.float32), jnp.where(at_power, power_row, 0.0))
+    facts = dot_nt(mine_half, facts_high) * 32.0 + dot_nt(mine_half, facts_low.astype(jnp.bfloat16))
+    facts = facts.astype(jnp.int32)
+
+    for c in range(slices):
+        columns = slice(c * LANES, (c + 1) * LANES)
+        placed = dot(place, jnp.concatenate([high[:, columns], low[:, columns]], axis=1))
+        placed = (placed[:, :LANES] * 256.0 + placed[:, LANES:]).astype(jnp.int32)
+        for j in range(words):
+            one = placed[j * groups : (j + 1) * groups]
+            two = placed[(j + words) * groups : (j + words + 1) * groups]
+            message_ref[pl.ds(c * share + j, groups, stride=block), :] = (one & 0xFFFF) | (two << 16)
+        message_ref[pl.ds(c * share + words, groups, stride=block), :] = facts
+
+    target = (owner * cap + position).astype(jnp.float32)
+    target = jnp.sum(jnp.where(on_diagonal, target, 0.0), axis=1, keepdims=True).astype(jnp.int32)
+    select_ref[...] = (iota((count, groups * cap), 1) == target).astype(jnp.bfloat16)
 
 
 def update_kernel(
@@ -104,7 +106,7 @@
         row = id_rows[s : s + 1]
         whole = (iota((coarse, sources), 0) == lax.div(row, fine)).astype(jnp.bfloat16)
         rest = (iota((fine, sources), 0) == lax.rem(row, fine)).astype(jnp.bfloat16)
-        counts = counts + lax.dot_general(whole, rest, (((1,), (1,)), ((), ())), preferred_element_type=jnp.float32)
+        counts = counts + dot_nt(whole, rest)
     counts = jnp.minimum(counts, 1.0).astype(jnp.bfloat16)
     whole = (lax.div(iota((own, coarse), 0), fine) == iota((own, coarse), 1)).astype(jnp.bfloat16)
     rest = lax.rem(iota((own, fine), 0), fine) == iota((own, fine), 1)
@@ -166,7 +168,12 @@
     cap = max(2, 2 * count // groups)
     block = cap // 2 + 1
     peers = groups * slices
-    items = jnp.concatenate([owners.reshape(1, count), local_ids.reshape(1, count)], axis=0)
+    steps_done = step_count[0].astype(jnp.float32)
+    fix_first = 1.0 - jnp.power(jnp.float32(0.9), steps_done)
+    fix_second = 1.0 - jnp.power(jnp.float32(0.999), steps_done)
+    fixes = jnp.stack([fix_first, fix_second])
+    names = jnp.concatenate([owners.reshape(1, count), local_ids.reshape(1, count)], axis=0)
+    names, fixes = lax.optimization_barrier((names, fixes))
     message, select = pl.pallas_call(
         functools.partial(pack_kernel, groups, cap, own),
         out_shape=(
@@ -177,13 +184,10 @@
         out_specs=(VMEM, VMEM),
         compiler_params=params_for(40),
         name="pack",
-    )(items, grads)
+    )(names, grads)
     message = message.reshape(peers, 1, block * lanes)
     message = lax.all_to_all(message, ORDER, split_axis=0, concat_axis=0, tiled=True)
     message = message.reshape(peers * block, lanes)
-    steps_done = step_count[0].astype(jnp.float32)
-    fix_first = 1.0 - jnp.power(jnp.float32(0.9), steps_done)
-    fix_second = 1.0 - jnp.power(jnp.float32(0.999), steps_done)
     table = jax.ShapeDtypeStruct((own, lanes), jnp.float32)
     new_params, new_first, new_second, answer = pl.pallas_call(
         functools.partial(update_kernel, cap),
@@ -197,7 +201,7 @@
         ],
         compiler_params=params_for(48),
         name="update",
-    )(message, jnp.stack([fix_first, fix_second]), params, first_moment, second_moment)
+    )(message, fixes, params, first_moment, second_moment)
     answer = answer.reshape(peers, cap, lanes)
     answer = lax.all_to_all(answer, ORDER, split_axis=0, concat_axis=0, tiled=True)
     row_steps = pl.pallas_call(

time: 119 us -> 118 us (level)
  blocking collectives: 43.2 us -> 105 us
  waiting for transfers between devices: 38.5 us -> 0 us
  starting transfers between devices: 22.2 us -> 0 us
  Pallas kernels: 11.3 us -> 9.85 us
    all_to_all x0 -> x1, blocking collectives: none -> 61.3 us  [local(): lax.all_to_all(message, ORDER, split_axis=0, concat_axis=0, tiled=True)]
    all_to_all x1 -> x0, waiting for transfers between devices: 38.5 us -> none  [local(): lax.all_to_all(message, ORDER, split_axis=0, concat_axis=0, tiled=True)]
    all_to_all x1 -> x0, starting transfers between devices: 22.2 us -> none  [local(): lax.all_to_all(message, ORDER, split_axis=0, concat_axis=0, tiled=True)]
    pallas_call x1, Pallas kernels: 3.02 us -> 1.57 us  [local(): pl.pallas_call(functools.partial(pack_kernel, groups, cap, own), out_shap...]
  transfers between devices with their start and end apart: 1 -> 0, of which waited for: 1 -> 0; matrix products, arithmetic and copies ran while one was open for 0% -> 0% of each run, Pallas kernels for 0% -> 0%
where the time goes in v3:
time: 118 us
  blocking collectives  105 us (89%)
  Pallas kernels  9.85 us (8%)
  between operations  1.41 us (1%)
  local copies, waits for them, and re-layouts  1.24 us (1%)
    all_to_all x1, blocking collectives, local(): lax.all_to_all(message, ORDER, split_axis=0, concat_axis=0, tiled=True)  61.3 us
    all_to_all x1, blocking collectives, local(): lax.all_to_all(answer, ORDER, split_axis=0, concat_axis=0, tiled=True)  43.2 us
    pallas_call x1, Pallas kernels, local(): pl.pallas_call(functools.partial(update_kernel, cap), out_shape=(table, t...  6.78 us

profile of v3, /device:TPU:1, one launch (start us, length us, event | category | flops | bytes accessed | tf_op | source)
XLA Modules:
  0.0 117.8 jit_solution(8928117624866268417)
XLA Ops:
  1.4 0.1 pad_maximum_fusion.fix_ref
  1.4 0.7 pad_add_fusion.names_ref
  2.1 0.0 copy-start
  2.1 1.2 %copy-done = f32[256,1024]{1,0:T(8,128)S(1)} copy-done((f32[256,1024]{1,0:T(8,128)S(1)}, f32[256,1024]{1,0:T(8,128)}, u32[]{:S(2)}) %copy-start) | copy-done | bytes 1048600
  3.4 1.6 %pack.1 = (s32[2560,128]{1,0:T(8,128)S(1)}, bf16[256,512]{1,0:T(8,128)(2,1)S(1)}) custom-call(s32[2,256]{1,0:T(2,128)S(1)} %pad_add_fusion.names_ref, f32[256,1024]{1,0:T(8,128)S(1)} %copy-done), custom_call_target="tpu_custom_call" | custom-call | tf_op jit(solution)/shard_map/pack/pallas_call | solution.py:177
  4.9 0.0 copy-start.1
  5.0 0.0 copy-start.2
  5.0 0.0 copy-start.3
  5.0 61.3 %all_to_all.10 = s32[512,1,640]{2,1,0:T(1,128)S(1)} all-to-all(s32[512,1,640]{2,1,0:T(1,128)S(1)} %bitcast.8), channel_id=1, replica_groups=mesh['rows'=64,'cols'=8] {'cols','rows'}, dimensions={0} | all-to-all | bytes 2621440 | tf_op jit(solution)/shard_map/all_to_all | solution.py:189
  66.3 0.0 copy-done.1
  66.3 0.0 copy-done.2
  66.3 0.0 copy-done.3
  66.3 6.8 %update.1 = (f32[1024,128]{1,0:T(8,128)}, f32[1024,128]{1,0:T(8,128)}, f32[1024,128]{1,0:T(8,128)}, bf16[4096,128]{1,0:T(8,128)(2,1)S(1)}) custom-call(s32[2560,128]{1,0:T(8,128)S(1)} %bitcast.6, f32[2]{0:T(128)S(1)} %pad_maximum_fusion.fix_ref, f32[1024,128]{1,0:T(8,128)S(1)} %copy-done.1, f32[1024,128]{1,0:T(8,128)S(1)} %copy-done.2, f32[1024,128]{1,0:T(8,128)S(1)} %copy-done.3), custom_call_target="tpu_custom_call" | custom-call | tf_op jit(solution)/shard_map/update/pallas_call | solution.py:192
  73.1 43.2 %all_to_all.11 = bf16[512,8,128]{2,1,0:T(8,128)(2,1)S(1)} all-to-all(bf16[512,8,128]{2,1,0:T(8,128)(2,1)S(1)} %bitcast.9), channel_id=1, replica_groups=mesh['rows'=64,'cols'=8] {'cols','rows'}, dimensions={0} | all-to-all | bytes 2097152 | tf_op jit(solution)/shard_map/all_to_all | solution.py:206
  116.3 1.5 %unpack.1 = bf16[256,1024]{1,0:T(8,128)(2,1)} custom-call(bf16[256,512]{1,0:T(8,128)(2,1)S(1)} %get-tuple-element.18.select_ref, bf16[4096,128]{1,0:T(8,128)(2,1)S(1)} %bitcast.7), custom_call_target="tpu_custom_call" | custom-call | tf_op jit(solution)/shard_map/unpack/pallas_call | solution.py:207
Async XLA Ops:
  2.1 1.2 %copy-start = (f32[256,1024]{1,0:T(8,128)S(1)}, f32[256,1024]{1,0:T(8,128)}, u32[]{:S(2)}) copy-start(f32[256,1024]{1,0:T(8,128)} %grads_ref.1) | copy-start | bytes 3145732
  4.9 61.4 %copy-start.1 = (f32[1024,128]{1,0:T(8,128)S(1)}, f32[1024,128]{1,0:T(8,128)}, u32[]{:S(2)}) copy-start(f32[1024,128]{1,0:T(8,128)} %params_ref.1) | copy-start | bytes 1572868
  5.0 61.3 %copy-start.2 = (f32[1024,128]{1,0:T(8,128)S(1)}, f32[1024,128]{1,0:T(8,128)}, u32[]{:S(2)}) copy-start(f32[1024,128]{1,0:T(8,128)} %first_ref.1) | copy-start | bytes 1572868
  5.0 61.3 %copy-start.3 = (f32[1024,128]{1,0:T(8,128)S(1)}, f32[1024,128]{1,0:T(8,128)}, u32[]{:S(2)}) copy-start(f32[1024,128]{1,0:T(8,128)} %second_ref.1) | copy-start | bytes 1572868

commit v4 on v3

--- a/solution.py
+++ b/solution.py
@@ -2,6 +2,7 @@
 
 import jax
 import jax.numpy as jnp
+import numpy as np
 from jax import lax
 from jax.experimental import pallas as pl
 from jax.experimental.pallas import tpu as pltpu
@@ -22,6 +23,16 @@
 
 def dot_nt(a, b):
     return lax.dot_general(a, b, (((1,), (1,)), ((), ())), preferred_element_type=jnp.float32)
+
+
+def one_minus_power(base, steps):
+    factor = 1.0 - float(np.float32(base))
+    total = jnp.float32(0.0)
+    for bit in range(5):
+        has = ((steps >> bit) & 1).astype(jnp.float32)
+        total = total + has * np.float32(factor) * (1.0 - total)
+        factor = factor * (2.0 - factor)
+    return total
 
 
 def pack_kernel(groups, cap, own, names_ref, grads_ref, message_ref, select_ref):
@@ -76,8 +87,8 @@
 
 
 def update_kernel(
-    cap, message_ref, fix_ref, params_ref, first_ref, second_ref,
-    new_params_hbm, new_first_hbm, new_second_hbm, answer_ref, spread_ref, table_ref, table_sem,
+    cap, message_ref, step_ref, params_ref, first_ref, second_ref,
+    new_params_hbm, new_first_hbm, new_second_hbm, answer_ref, spread_ref, halves_ref, table_ref, table_sem,
 ):
     own, lanes = params_ref.shape
     words = cap // 2
@@ -112,10 +123,12 @@
     rest = lax.rem(iota((own, fine), 0), fine) == iota((own, fine), 1)
     live = jnp.sum(jnp.where(rest, dot(whole, counts), 0.0), axis=1, keepdims=True) > 0.0
     summed = (total[:, :lanes] + total[:, lanes:]) * (1.0 / (FULL * FULL))
+    fix_first = one_minus_power(0.9, step_ref[0])
+    fix_second = one_minus_power(0.999, step_ref[0])
     first, second, params = first_ref[...], second_ref[...], params_ref[...]
     new_first = jnp.where(live, 0.9 * first + 0.1 * summed, first)
     new_second = jnp.where(live, 0.999 * second + 0.001 * summed * summed, second)
-    direction = -(new_first / fix_ref[0]) / (jnp.sqrt(new_second / fix_ref[1]) + 1e-08)
+    direction = -(new_first / fix_first) / (jnp.sqrt(new_second / fix_second) + 1e-08)
     table_ref[0] = jnp.where(live, params + 0.01 * direction, params)
     table_ref[1] = new_first
     table_ref[2] = new_second
@@ -128,27 +141,41 @@
 
     half = own // 2
     direction = direction.astype(jnp.bfloat16)
-    table = jnp.concatenate([direction[:half], direction[half:]], axis=1)
-    spots = iota((sources, half), 1).astype(jnp.int16)
-    ids = facts - 1
-    for s in range(cap):
-        wanted = jnp.broadcast_to(ids[:, s : s + 1], (sources, lanes))
+    halves_ref[...] = jnp.concatenate([direction[:half], direction[half:]], axis=1)
+    part = sources // 2
+    spots = iota((cap * part, half), 1).astype(jnp.int16)
+
+    def answer_part(p, carry):
+        ids = message_ref[pl.ds(p * part * block + words, part, stride=block), :] - 1
+        wanted = jnp.concatenate([jnp.broadcast_to(ids[:, s : s + 1], (part, lanes)) for s in range(cap)], axis=0)
         upper = wanted >= half
         spot = jnp.where(upper, wanted - half, wanted).astype(jnp.int16)
         hit = (spots == jnp.concatenate([spot] * (half // lanes), axis=1)).astype(jnp.bfloat16)
-        both = dot(hit, table)
-        spread_ref[pl.ds(s, sources, stride=cap), :] = jnp.where(upper, both[:, lanes:], both[:, :lanes])
-    answer_ref[...] = spread_ref[...].astype(jnp.bfloat16)
+        both = dot(hit, halves_ref[...])
+        found = jnp.where(upper, both[:, lanes:], both[:, :lanes])
+        for s in range(cap):
+            spread_ref[pl.ds(p * part * cap + s, part, stride=cap), :] = found[s * part : (s + 1) * part]
+        rows = pl.ds(pl.multiple_of(p * part * cap, part * cap), part * cap)
+        answer_ref[rows, :] = spread_ref[rows, :].astype(jnp.bfloat16)
+        return carry
+
+    lax.fori_loop(0, 2, answer_part, 0)
     for copy in copies:
         copy.wait()
 
 
-def unpack_kernel(select_ref, back_ref, out_ref):
+def unpack_kernel(select_ref, back_ref, out_hbm, out_ref, out_sem):
     select = select_ref[...]
     slots = select.shape[1]
+    copies = []
     for c in range(out_ref.shape[1] // LANES):
+        columns = pl.ds(c * LANES, LANES)
         rows = dot(select, back_ref[c * slots : (c + 1) * slots])
-        out_ref[:, c * LANES : (c + 1) * LANES] = rows.astype(jnp.bfloat16)
+        out_ref[:, columns] = rows.astype(jnp.bfloat16)
+        copies.append(pltpu.make_async_copy(out_ref.at[:, columns], out_hbm.at[:, columns], out_sem.at[c]))
+        copies[-1].start()
+    for copy in copies:
+        copy.wait()
 
 
 VMEM = pl.BlockSpec(memory_space=pltpu.VMEM)
@@ -168,12 +195,7 @@
     cap = max(2, 2 * count // groups)
     block = cap // 2 + 1
     peers = groups * slices
-    steps_done = step_count[0].astype(jnp.float32)
-    fix_first = 1.0 - jnp.power(jnp.float32(0.9), steps_done)
-    fix_second = 1.0 - jnp.power(jnp.float32(0.999), steps_done)
-    fixes = jnp.stack([fix_first, fix_second])
     names = jnp.concatenate([owners.reshape(1, count), local_ids.reshape(1, count)], axis=0)
-    names, fixes = lax.optimization_barrier((names, fixes))
     message, select = pl.pallas_call(
         functools.partial(pack_kernel, groups, cap, own),
         out_shape=(
@@ -196,19 +218,21 @@
         out_specs=(HBM, HBM, HBM, VMEM),
         scratch_shapes=[
             pltpu.VMEM((peers * cap, lanes), jnp.float32),
+            pltpu.VMEM((own // 2, 2 * lanes), jnp.bfloat16),
             pltpu.VMEM((3, own, lanes), jnp.float32),
             pltpu.SemaphoreType.DMA((3,)),
         ],
         compiler_params=params_for(48),
         name="update",
-    )(message, fixes, params, first_moment, second_moment)
+    )(message, step_count, params, first_moment, second_moment)
     answer = answer.reshape(peers, cap, lanes)
     answer = lax.all_to_all(answer, ORDER, split_axis=0, concat_axis=0, tiled=True)
     row_steps = pl.pallas_call(
         unpack_kernel,
         out_shape=jax.ShapeDtypeStruct((count, width), jnp.bfloat16),
         in_specs=[VMEM, VMEM],
-        out_specs=VMEM,
+        out_specs=HBM,
+        scratch_shapes=[pltpu.VMEM((count, width), jnp.bfloat16), pltpu.SemaphoreType.DMA((slices,))],
         compiler_params=params_for(40),
         name="unpack",
     )(select, answer.reshape(peers * cap, lanes))

time: 118 us -> 117 us (level)
  blocking collectives: 105 us -> 43 us
  waiting for transfers between devices: 0 us -> 38.7 us
  starting transfers between devices: 0 us -> 22.2 us
    all_to_all x1 -> x0, blocking collectives: 61.3 us -> none  [local(): lax.all_to_all(message, ORDER, split_axis=0, concat_axis=0, tiled=True)]
    all_to_all x0 -> x1, waiting for transfers between devices: none -> 38.7 us  [local(): lax.all_to_all(message, ORDER, split_axis=0, concat_axis=0, tiled=True)]
    all_to_all x0 -> x1, starting transfers between devices: none -> 22.2 us  [local(): lax.all_to_all(message, ORDER, split_axis=0, concat_axis=0, tiled=True)]
    pallas_call x1, Pallas kernels: 6.78 us -> 5.36 us  [local(): pl.pallas_call(functools.partial(update_kernel, cap), out_shape=(table, t...]
  transfers between devices with their start and end apart: 0 -> 1, of which waited for: 0 -> 1; matrix products, arithmetic and copies ran while one was open for 0% -> 0% of each run, Pallas kernels for 0% -> 0%
where the time goes in v4:
time: 117 us
  blocking collectives  43 us (37%)
  waiting for transfers between devices  38.7 us (33%)
  starting transfers between devices  22.2 us (19%)
  Pallas kernels  9.4 us (8%)
  between operations  1.3 us (1%)
  local copies, waits for them, and re-layouts  1.24 us (1%)
    all_to_all x1, blocking collectives, local(): lax.all_to_all(answer, ORDER, split_axis=0, concat_axis=0, tiled=True)  43 us
    all_to_all x1, waiting for transfers between devices, local(): lax.all_to_all(message, ORDER, split_axis=0, concat_axis=0, tiled=True)  38.7 us
    all_to_all x1, starting transfers between devices, local(): lax.all_to_all(message, ORDER, split_axis=0, concat_axis=0, tiled=True)  22.2 us
    pallas_call x1, Pallas kernels, local(): pl.pallas_call(functools.partial(update_kernel, cap), out_shape=(table, t...  5.36 us
    pallas_call x1, Pallas kernels, local(): pl.pallas_call(functools.partial(pack_kernel, groups, cap, own), out_shap...  2.64 us
  transfers between devices with their start and end apart: 1, of which 1 were waited for; matrix products, arithmetic and copies ran while one was open for 0% of the time, Pallas kernels for 0%

profile of v4, /device:TPU:1, one launch (start us, length us, event | category | flops | bytes accessed | tf_op | source)
XLA Modules:
  0.0 116.5 jit_solution(16535411880891076775)
XLA Ops:
  0.6 0.7 pad_add_fusion.names_ref
  1.3 0.0 copy-start
  1.3 1.2 %copy-done = f32[256,1024]{1,0:T(8,128)S(1)} copy-done((f32[256,1024]{1,0:T(8,128)S(1)}, f32[256,1024]{1,0:T(8,128)}, u32[]{:S(2)}) %copy-start) | copy-done | bytes 1048600
  2.6 2.6 %pack.1 = (s32[2560,128]{1,0:T(8,128)}, bf16[256,512]{1,0:T(8,128)(2,1)S(1)}) custom-call(s32[2,256]{1,0:T(2,128)S(1)} %pad_add_fusion.names_ref, f32[256,1024]{1,0:T(8,128)S(1)} %copy-done), custom_call_target="tpu_custom_call" | custom-call | tf_op jit(solution)/shard_map/pack/pallas_call | solution.py:199
  5.2 0.0 copy-start.1
  5.2 0.0 copy-start.2
  5.2 0.0 copy-start.3
  5.2 22.2 %all-to-all-start = ((s32[512,1,640]{2,1,0:T(1,128)}), s32[512,1,640]{2,1,0:T(1,128)S(1)}, u32[]{:S(2)}, u32[]{:S(2)}) async-start(s32[512,1,640]{2,1,0:T(1,128)} %bitcast.2), calls=%async_computation | async-start | bytes 2621440 | tf_op jit(solution)/shard_map/all_to_all | solution.py:211
  28.0 38.7 %all-to-all-done = s32[512,1,640]{2,1,0:T(1,128)S(1)} async-done(((s32[512,1,640]{2,1,0:T(1,128)}), s32[512,1,640]{2,1,0:T(1,128)S(1)}, u32[]{:S(2)}, u32[]{:S(2)}) %all-to-all-start) | async-done | bytes 1310752 | tf_op jit(solution)/shard_map/all_to_all | solution.py:211
  66.7 0.0 copy-done.1
  66.7 0.0 copy-done.2
  66.7 0.0 copy-done.3
  66.7 5.4 %update.1 = (f32[1024,128]{1,0:T(8,128)}, f32[1024,128]{1,0:T(8,128)}, f32[1024,128]{1,0:T(8,128)}, bf16[4096,128]{1,0:T(8,128)(2,1)S(1)}) custom-call(s32[2560,128]{1,0:T(8,128)S(1)} %bitcast.6, s32[1]{0:T(128)S(6)} %copy.12.step_ref, f32[1024,128]{1,0:T(8,128)S(1)} %copy-done.1, f32[1024,128]{1,0:T(8,128)S(1)} %copy-done.2, f32[1024,128]{1,0:T(8,128)S(1)} %copy-done.3), custom_call_target="tpu_custom_call" | custom-call | tf_op jit(solution)/shard_map/update/pallas_call | solution.py:214
  72.1 43.0 %all_to_all.10 = bf16[512,8,128]{2,1,0:T(8,128)(2,1)S(1)} all-to-all(bf16[512,8,128]{2,1,0:T(8,128)(2,1)S(1)} %bitcast.8), channel_id=1, replica_groups=mesh['rows'=64,'cols'=8] {'cols','rows'}, dimensions={0} | all-to-all | bytes 2097152 | tf_op jit(solution)/shard_map/all_to_all | solution.py:229
  115.1 1.4 %unpack.1 = bf16[256,1024]{1,0:T(8,128)(2,1)} custom-call(bf16[256,512]{1,0:T(8,128)(2,1)S(1)} %get-tuple-element.14.select_ref, bf16[4096,128]{1,0:T(8,128)(2,1)S(1)} %bitcast.7), custom_call_target="tpu_custom_call" | custom-call | tf_op jit(solution)/shard_map/unpack/pallas_call | solution.py:230
Async XLA Ops:
  1.3 1.2 %copy-start = (f32[256,1024]{1,0:T(8,128)S(1)}, f32[256,1024]{1,0:T(8,128)}, u32[]{:S(2)}) copy-start(f32[256,1024]{1,0:T(8,128)} %grads_ref.1) | copy-start | bytes 3145732
  5.2 61.5 %copy-start.1 = (f32[1024,128]{1,0:T(8,128)S(1)}, f32[1024,128]{1,0:T(8,128)}, u32[]{:S(2)}) copy-start(f32[1024,128]{1,0:T(8,128)} %params_ref.1) | copy-start | bytes 1572868
  5.2 61.5 %copy-start.2 = (f32[1024,128]{1,0:T(8,128)S(1)}, f32[1024,128]{1,0:T(8,128)}, u32[]{:S(2)}) copy-start(f32[1024,128]{1,0:T(8,128)} %first_ref.1) | copy-start | bytes 1572868
  5.2 61.5 %copy-start.3 = (f32[1024,128]{1,0:T(8,128)S(1)}, f32[1024,128]{1,0:T(8,128)}, u32[]{:S(2)}) copy-start(f32[1024,128]{1,0:T(8,128)} %second_ref.1) | copy-start | bytes 1572868
  5.2 61.5 %all-to-all-start = ((s32[512,1,640]{2,1,0:T(1,128)}), s32[512,1,640]{2,1,0:T(1,128)S(1)}, u32[]{:S(2)}, u32[]{:S(2)}) async-start(s32[512,1,640]{2,1,0:T(1,128)} %bitcast.2), calls=%async_computation | async-start | bytes 2621440 | tf_op jit(solution)/shard_map/all_to_all | solution.py:211

commit v5 on v4

--- a/solution.py
+++ b/solution.py
@@ -27,7 +27,7 @@
 
 def one_minus_power(base, steps):
     factor = 1.0 - float(np.float32(base))
-    total = jnp.float32(0.0)
+    total = jnp.zeros_like(steps, jnp.float32)
     for bit in range(5):
         has = ((steps >> bit) & 1).astype(jnp.float32)
         total = total + has * np.float32(factor) * (1.0 - total)
@@ -123,8 +123,8 @@
     rest = lax.rem(iota((own, fine), 0), fine) == iota((own, fine), 1)
     live = jnp.sum(jnp.where(rest, dot(whole, counts), 0.0), axis=1, keepdims=True) > 0.0
     summed = (total[:, :lanes] + total[:, lanes:]) * (1.0 / (FULL * FULL))
-    fix_first = one_minus_power(0.9, step_ref[0])
-    fix_second = one_minus_power(0.999, step_ref[0])
+    fix_first = one_minus_power(0.9, step_ref[...])
+    fix_second = one_minus_power(0.999, step_ref[...])
     first, second, params = first_ref[...], second_ref[...], params_ref[...]
     new_first = jnp.where(live, 0.9 * first + 0.1 * summed, first)
     new_second = jnp.where(live, 0.999 * second + 0.001 * summed * summed, second)
@@ -180,7 +180,6 @@
 
 VMEM = pl.BlockSpec(memory_space=pltpu.VMEM)
 HBM = pl.BlockSpec(memory_space=pltpu.HBM)
-SMEM = pl.BlockSpec(memory_space=pltpu.SMEM)
 
 
 def params_for(mib):
@@ -214,7 +213,7 @@
     new_params, new_first, new_second, answer = pl.pallas_call(
         functools.partial(update_kernel, cap),
         out_shape=(table, table, table, jax.ShapeDtypeStruct((peers * cap, lanes), jnp.bfloat16)),
-        in_specs=[VMEM, SMEM, VMEM, VMEM, VMEM],
+        in_specs=[VMEM, VMEM, VMEM, VMEM, VMEM],
         out_specs=(HBM, HBM, HBM, VMEM),
         scratch_shapes=[
             pltpu.VMEM((peers * cap, lanes), jnp.float32),
@@ -224,7 +223,7 @@
         ],
         compiler_params=params_for(48),
         name="update",
-    )(message, step_count, params, first_moment, second_moment)
+    )(message, step_count.reshape(1, 1), params, first_moment, second_moment)
     answer = answer.reshape(peers, cap, lanes)
     answer = lax.all_to_all(answer, ORDER, split_axis=0, concat_axis=0, tiled=True)
     row_steps = pl.pallas_call(

time: 117 us -> 117 us (level)
  no operation moved by 1% of the time
where the time goes in v5:
time: 117 us
  blocking collectives  43 us (37%)
  waiting for transfers between devices  38.7 us (33%)
  starting transfers between devices  22.2 us (19%)
  Pallas kernels  9.52 us (8%)
  between operations  1.3 us (1%)
  local copies, waits for them, and re-layouts  1.24 us (1%)
    all_to_all x1, blocking collectives, local(): lax.all_to_all(answer, ORDER, split_axis=0, concat_axis=0, tiled=True)  43 us
    all_to_all x1, waiting for transfers between devices, local(): lax.all_to_all(message, ORDER, split_axis=0, concat_axis=0, tiled=True)  38.7 us
    all_to_all x1, starting transfers between devices, local(): lax.all_to_all(message, ORDER, split_axis=0, concat_axis=0, tiled=True)  22.2 us
    pallas_call x1, Pallas kernels, local(): pl.pallas_call(functools.partial(update_kernel, cap), out_shape=(table, t...  5.48 us
    pallas_call x1, Pallas kernels, local(): pl.pallas_call(functools.partial(pack_kernel, groups, cap, own), out_shap...  2.64 us
  transfers between devices with their start and end apart: 1, of which 1 were waited for; matrix products, arithmetic and copies ran while one was open for 0% of the time, Pallas kernels for 0%

profile of v5, /device:TPU:1, one launch (start us, length us, event | category | flops | bytes accessed | tf_op | source)
XLA Modules:
  0.0 116.6 jit_solution(16232406509661622953)
XLA Ops:
  0.6 0.7 pad_add_fusion.names_ref
  1.3 0.0 copy-start
  1.3 1.2 %copy-done = f32[256,1024]{1,0:T(8,128)S(1)} copy-done((f32[256,1024]{1,0:T(8,128)S(1)}, f32[256,1024]{1,0:T(8,128)}, u32[]{:S(2)}) %copy-start) | copy-done | bytes 1048600
  2.6 2.6 %pack.1 = (s32[2560,128]{1,0:T(8,128)}, bf16[256,512]{1,0:T(8,128)(2,1)S(1)}) custom-call(s32[2,256]{1,0:T(2,128)S(1)} %pad_add_fusion.names_ref, f32[256,1024]{1,0:T(8,128)S(1)} %copy-done), custom_call_target="tpu_custom_call" | custom-call | tf_op jit(solution)/shard_map/pack/pallas_call | solution.py:198
  5.2 0.0 copy-start.1
  5.2 0.0 copy-start.2
  5.2 0.0 copy-start.3
  5.2 22.2 %all-to-all-start = ((s32[512,1,640]{2,1,0:T(1,128)}), s32[512,1,640]{2,1,0:T(1,128)S(1)}, u32[]{:S(2)}, u32[]{:S(2)}) async-start(s32[512,1,640]{2,1,0:T(1,128)} %bitcast.2), calls=%async_computation | async-start | bytes 2621440 | tf_op jit(solution)/shard_map/all_to_all | solution.py:210
  28.0 38.7 %all-to-all-done = s32[512,1,640]{2,1,0:T(1,128)S(1)} async-done(((s32[512,1,640]{2,1,0:T(1,128)}), s32[512,1,640]{2,1,0:T(1,128)S(1)}, u32[]{:S(2)}, u32[]{:S(2)}) %all-to-all-start) | async-done | bytes 1310752 | tf_op jit(solution)/shard_map/all_to_all | solution.py:210
  66.7 0.0 copy-done.1
  66.7 0.0 copy-done.2
  66.7 0.0 copy-done.3
  66.7 5.5 %update.1 = (f32[1024,128]{1,0:T(8,128)}, f32[1024,128]{1,0:T(8,128)}, f32[1024,128]{1,0:T(8,128)}, bf16[4096,128]{1,0:T(8,128)(2,1)S(1)}) custom-call(s32[2560,128]{1,0:T(8,128)S(1)} %bitcast.8, s32[1,1]{1,0:T(1,128)} %bitcast.7.step_ref, f32[1024,128]{1,0:T(8,128)S(1)} %copy-done.1, f32[1024,128]{1,0:T(8,128)S(1)} %copy-done.2, f32[1024,128]{1,0:T(8,128)S(1)} %copy-done.3), custom_call_target="tpu_custom_call" | custom-call | tf_op jit(solution)/shard_map/update/pallas_call | solution.py:213
  72.2 43.0 %all_to_all.10 = bf16[512,8,128]{2,1,0:T(8,128)(2,1)S(1)} all-to-all(bf16[512,8,128]{2,1,0:T(8,128)(2,1)S(1)} %bitcast.10), channel_id=1, replica_groups=mesh['rows'=64,'cols'=8] {'cols','rows'}, dimensions={0} | all-to-all | bytes 2097152 | tf_op jit(solution)/shard_map/all_to_all | solution.py:228
  115.2 1.4 %unpack.1 = bf16[256,1024]{1,0:T(8,128)(2,1)} custom-call(bf16[256,512]{1,0:T(8,128)(2,1)S(1)} %get-tuple-element.14.select_ref, bf16[4096,128]{1,0:T(8,128)(2,1)S(1)} %bitcast.9), custom_call_target="tpu_custom_call" | custom-call | tf_op jit(solution)/shard_map/unpack/pallas_call | solution.py:229
Async XLA Ops:
  1.3 1.2 %copy-start = (f32[256,1024]{1,0:T(8,128)S(1)}, f32[256,1024]{1,0:T(8,128)}, u32[]{:S(2)}) copy-start(f32[256,1024]{1,0:T(8,128)} %grads_ref.1) | copy-start | bytes 3145732
  5.2 61.5 %copy-start.1 = (f32[1024,128]{1,0:T(8,128)S(1)}, f32[1024,128]{1,0:T(8,128)}, u32[]{:S(2)}) copy-start(f32[1024,128]{1,0:T(8,128)} %params_ref.1) | copy-start | bytes 1572868
  5.2 61.5 %copy-start.2 = (f32[1024,128]{1,0:T(8,128)S(1)}, f32[1024,128]{1,0:T(8,128)}, u32[]{:S(2)}) copy-start(f32[1024,128]{1,0:T(8,128)} %first_ref.1) | copy-start | bytes 1572868
  5.2 61.5 %copy-start.3 = (f32[1024,128]{1,0:T(8,128)S(1)}, f32[1024,128]{1,0:T(8,128)}, u32[]{:S(2)}) copy-start(f32[1024,128]{1,0:T(8,128)} %second_ref.1) | copy-start | bytes 1572868
  5.2 61.5 %all-to-all-start = ((s32[512,1,640]{2,1,0:T(1,128)}), s32[512,1,640]{2,1,0:T(1,128)S(1)}, u32[]{:S(2)}, u32[]{:S(2)}) async-start(s32[512,1,640]{2,1,0:T(1,128)} %bitcast.2), calls=%async_computation | async-start | bytes 2621440 | tf_op jit(solution)/shard_map/all_to_all | solution.py:210

commit v6 on v5

--- a/solution.py
+++ b/solution.py
@@ -35,13 +35,27 @@
     return total
 
 
-def pack_kernel(groups, cap, own, names_ref, grads_ref, message_ref, select_ref):
+def pack_kernel(
+    groups, cap, owners_hbm, ids_hbm, grads_hbm, message_hbm, select_hbm,
+    owners_ref, ids_ref, grads_ref, message_ref, select_ref, names_sem, grads_sem, message_sem, select_sem,
+):
     count, width = grads_ref.shape
     words = cap // 2
     block = words + 1
     slices = width // LANES
     share = groups * block
-    owner = names_ref[0:1]
+    names = [
+        pltpu.make_async_copy(owners_hbm, owners_ref, names_sem.at[0]),
+        pltpu.make_async_copy(ids_hbm, ids_ref, names_sem.at[1]),
+    ]
+    load = pltpu.make_async_copy(grads_hbm, grads_ref, grads_sem)
+    for copy in names:
+        copy.start()
+    load.start()
+    for copy in names:
+        copy.wait()
+
+    owner = owners_ref[...]
     mine = owner == iota((groups, count), 0)
     mine_half = mine.astype(jnp.bfloat16)
     square = (count, count)
@@ -51,6 +65,13 @@
     place = (iota((groups * cap, count), 0) == position * groups + owner).astype(jnp.bfloat16)
     on_diagonal = iota(square, 0) == iota(square, 1)
 
+    target = (owner * cap + position).astype(jnp.float32)
+    target = jnp.sum(jnp.where(on_diagonal, target, 0.0), axis=1, keepdims=True).astype(jnp.int32)
+    select_ref[...] = (iota((count, groups * cap), 1) == target).astype(jnp.bfloat16)
+    stores = [pltpu.make_async_copy(select_ref, select_hbm, select_sem)]
+    stores[0].start()
+
+    load.wait()
     grads = grads_ref[...]
     size = jnp.abs(grads)
     top = jnp.max(size, axis=1, keepdims=True)
@@ -62,7 +83,7 @@
     high = high.astype(jnp.bfloat16)
 
     power_row = jnp.sum(jnp.where(on_diagonal, power, 0.0), axis=0, keepdims=True)
-    named = names_ref[1:2] + 1
+    named = ids_ref[...] + 1
     lane = iota((LANES, count), 0)
     at_id = lane == position
     at_power = lane == position + cap
@@ -80,10 +101,12 @@
             two = placed[(j + words) * groups : (j + words + 1) * groups]
             message_ref[pl.ds(c * share + j, groups, stride=block), :] = (one & 0xFFFF) | (two << 16)
         message_ref[pl.ds(c * share + words, groups, stride=block), :] = facts
-
-    target = (owner * cap + position).astype(jnp.float32)
-    target = jnp.sum(jnp.where(on_diagonal, target, 0.0), axis=1, keepdims=True).astype(jnp.int32)
-    select_ref[...] = (iota((count, groups * cap), 1) == target).astype(jnp.bfloat16)
+        rows = pl.ds(c * share, share)
+        stores.append(pltpu.make_async_copy(message_ref.at[rows], message_hbm.at[rows], message_sem.at[c]))
+        stores[-1].start()
+
+    for copy in stores:
+        copy.wait()
 
 
 def update_kernel(
@@ -194,18 +217,28 @@
     cap = max(2, 2 * count // groups)
     block = cap // 2 + 1
     peers = groups * slices
-    names = jnp.concatenate([owners.reshape(1, count), local_ids.reshape(1, count)], axis=0)
     message, select = pl.pallas_call(
-        functools.partial(pack_kernel, groups, cap, own),
+        functools.partial(pack_kernel, groups, cap),
         out_shape=(
             jax.ShapeDtypeStruct((peers * block, lanes), jnp.int32),
             jax.ShapeDtypeStruct((count, groups * cap), jnp.bfloat16),
         ),
-        in_specs=[VMEM, VMEM],
-        out_specs=(VMEM, VMEM),
-        compiler_params=params_for(40),
+        in_specs=[HBM, HBM, HBM],
+        out_specs=(HBM, HBM),
+        scratch_shapes=[
+            pltpu.VMEM((1, count), jnp.int32),
+            pltpu.VMEM((1, count), jnp.int32),
+            pltpu.VMEM((count, width), jnp.float32),
+            pltpu.VMEM((peers * block, lanes), jnp.int32),
+            pltpu.VMEM((count, groups * cap), jnp.bfloat16),
+            pltpu.SemaphoreType.DMA((2,)),
+            pltpu.SemaphoreType.DMA,
+            pltpu.SemaphoreType.DMA((slices,)),
+            pltpu.SemaphoreType.DMA,
+        ],
+        compiler_params=params_for(56),
         name="pack",
-    )(names, grads)
+    )(owners.reshape(1, count), local_ids.reshape(1, count), grads)
     message = message.reshape(peers, 1, block * lanes)
     message = lax.all_to_all(message, ORDER, split_axis=0, concat_axis=0, tiled=True)
     message = message.reshape(peers * block, lanes)

time: 117 us -> 116 us (level)
  local copies, waits for them, and re-layouts: 1.24 us -> 0.03 us
    unnamed x8, local copies, waits for them, and re-layouts: 1.24 us -> 0.03 us
where the time goes in v6:
time: 116 us
  blocking collectives  43.2 us (37%)
  waiting for transfers between devices  38.7 us (33%)
  starting transfers between devices  22.2 us (19%)
  Pallas kernels  10.4 us (9%)
  between operations  1.34 us (1%)
    all_to_all x1, blocking collectives, local(): lax.all_to_all(answer, ORDER, split_axis=0, concat_axis=0, tiled=True)  43.2 us
    all_to_all x1, waiting for transfers between devices, local(): lax.all_to_all(message, ORDER, split_axis=0, concat_axis=0, tiled=True)  38.7 us
    all_to_all x1, starting transfers between devices, local(): lax.all_to_all(message, ORDER, split_axis=0, concat_axis=0, tiled=True)  22.2 us
    pallas_call x1, Pallas kernels, local(): pl.pallas_call(functools.partial(update_kernel, cap), out_shape=(table, t...  5.48 us
    pallas_call x1, Pallas kernels, local(): pl.pallas_call(functools.partial(pack_kernel, groups, cap), out_shape=(ja...  3.5 us
  transfers between devices with their start and end apart: 1, of which 1 were waited for; matrix products, arithmetic and copies ran while one was open for 0% of the time, Pallas kernels for 0%

profile of v6, /device:TPU:1, one launch (start us, length us, event | category | flops | bytes accessed | tf_op | source)
XLA Modules:
  0.0 115.8 jit_solution(17111621070990114950)
XLA Ops:
  0.6 3.5 %pack.1 = (s32[2560,128]{1,0:T(8,128)}, bf16[256,512]{1,0:T(8,128)(2,1)}) custom-call(s32[1,256]{1,0:T(1,128)} %bitcast.12, s32[1,256]{1,0:T(1,128)} %bitcast.13, f32[256,1024]{1,0:T(8,128)} %grads_hbm.1), custom_call_target="tpu_custom_call" | custom-call | tf_op jit(solution)/shard_map/pack/pallas_call | solution.py:220
  4.1 0.0 copy-start
  4.2 0.0 copy-start.1
  4.2 0.0 copy-start.2
  4.2 22.2 %all-to-all-start = ((s32[512,1,640]{2,1,0:T(1,128)}), s32[512,1,640]{2,1,0:T(1,128)S(1)}, u32[]{:S(2)}, u32[]{:S(2)}) async-start(s32[512,1,640]{2,1,0:T(1,128)} %bitcast.11), calls=%async_computation | async-start | bytes 2621440 | tf_op jit(solution)/shard_map/all_to_all | solution.py:243
  27.0 38.7 %all-to-all-done = s32[512,1,640]{2,1,0:T(1,128)S(1)} async-done(((s32[512,1,640]{2,1,0:T(1,128)}), s32[512,1,640]{2,1,0:T(1,128)S(1)}, u32[]{:S(2)}, u32[]{:S(2)}) %all-to-all-start) | async-done | bytes 1310752 | tf_op jit(solution)/shard_map/all_to_all | solution.py:243
  65.7 0.0 copy-done
  65.7 0.0 copy-done.1
  65.7 0.0 copy-done.2
  65.7 5.5 %update.1 = (f32[1024,128]{1,0:T(8,128)}, f32[1024,128]{1,0:T(8,128)}, f32[1024,128]{1,0:T(8,128)}, bf16[4096,128]{1,0:T(8,128)(2,1)S(1)}) custom-call(s32[2560,128]{1,0:T(8,128)S(1)} %bitcast.8, s32[1,1]{1,0:T(1,128)} %bitcast.7.step_ref, f32[1024,128]{1,0:T(8,128)S(1)} %copy-done, f32[1024,128]{1,0:T(8,128)S(1)} %copy-done.1, f32[1024,128]{1,0:T(8,128)S(1)} %copy-done.2), custom_call_target="tpu_custom_call" | custom-call | tf_op jit(solution)/shard_map/update/pallas_call | solution.py:246
  71.2 0.0 copy-start.3
  71.2 43.2 %all_to_all.10 = bf16[512,8,128]{2,1,0:T(8,128)(2,1)S(1)} all-to-all(bf16[512,8,128]{2,1,0:T(8,128)(2,1)S(1)} %bitcast.10), channel_id=1, replica_groups=mesh['rows'=64,'cols'=8] {'cols','rows'}, dimensions={0} | all-to-all | bytes 2097152 | tf_op jit(solution)/shard_map/all_to_all | solution.py:261
  114.4 0.0 copy-done.3
  114.4 1.4 %unpack.1 = bf16[256,1024]{1,0:T(8,128)(2,1)} custom-call(bf16[256,512]{1,0:T(8,128)(2,1)S(1)} %copy-done.3, bf16[4096,128]{1,0:T(8,128)(2,1)S(1)} %bitcast.9), custom_call_target="tpu_custom_call" | custom-call | tf_op jit(solution)/shard_map/unpack/pallas_call | solution.py:262
Async XLA Ops:
  4.1 61.6 %copy-start = (f32[1024,128]{1,0:T(8,128)S(1)}, f32[1024,128]{1,0:T(8,128)}, u32[]{:S(2)}) copy-start(f32[1024,128]{1,0:T(8,128)} %params_ref.1) | copy-start | bytes 1572868
  4.2 61.6 %copy-start.1 = (f32[1024,128]{1,0:T(8,128)S(1)}, f32[1024,128]{1,0:T(8,128)}, u32[]{:S(2)}) copy-start(f32[1024,128]{1,0:T(8,128)} %first_ref.1) | copy-start | bytes 1572868
  4.2 61.5 %copy-start.2 = (f32[1024,128]{1,0:T(8,128)S(1)}, f32[1024,128]{1,0:T(8,128)}, u32[]{:S(2)}) copy-start(f32[1024,128]{1,0:T(8,128)} %second_ref.1) | copy-start | bytes 1572868
  4.2 61.5 %all-to-all-start = ((s32[512,1,640]{2,1,0:T(1,128)}), s32[512,1,640]{2,1,0:T(1,128)S(1)}, u32[]{:S(2)}, u32[]{:S(2)}) async-start(s32[512,1,640]{2,1,0:T(1,128)} %bitcast.11), calls=%async_computation | async-start | bytes 2621440 | tf_op jit(solution)/shard_map/all_to_all | solution.py:243
  71.2 43.2 %copy-start.3 = (bf16[256,512]{1,0:T(8,128)(2,1)S(1)}, bf16[256,512]{1,0:T(8,128)(2,1)}, u32[]{:S(2)}) copy-start(bf16[256,512]{1,0:T(8,128)(2,1)} %get-tuple-element.14.select_ref) | copy-start | bytes 786436

commit v7 on v6

--- a/solution.py
+++ b/solution.py
@@ -10,6 +10,8 @@
 
 LANES = 128
 FULL = 32767.0
+TINY = 1e-30
+SPARE = 8
 ORDER = ("cols", "rows")
 
 
@@ -75,7 +77,7 @@
     grads = grads_ref[...]
     size = jnp.abs(grads)
     top = jnp.max(size, axis=1, keepdims=True)
-    power = jnp.clip(jnp.ceil(jnp.log2(top)), -120.0, 100.0)
+    power = jnp.ceil(jnp.log2(jnp.maximum(top, TINY)))
     code = jnp.minimum(jnp.floor(jnp.sqrt(size * jnp.exp2(-power)) * FULL + 0.5), FULL)
     code = jnp.where(grads < 0.0, -code, code)
     high = jnp.floor(code * (1.0 / 256.0) + 0.5)
@@ -111,13 +113,22 @@
 
 def update_kernel(
     cap, message_ref, step_ref, params_ref, first_ref, second_ref,
-    new_params_hbm, new_first_hbm, new_second_hbm, answer_ref, spread_ref, halves_ref, table_ref, table_sem,
+    new_params_hbm, new_first_hbm, new_second_hbm, answer_ref,
+    tail_ref, facts_ref, spread_ref, halves_ref, table_ref, table_sem,
 ):
     own, lanes = params_ref.shape
     words = cap // 2
     block = words + 1
     sources = message_ref.shape[0] // block
-    facts = message_ref[pl.ds(words, sources, stride=block), :]
+    tail = SPARE * block
+    tail_ref[:tail] = message_ref[sources * block - tail :]
+
+    def row(j):
+        most = message_ref[pl.ds(j, sources - SPARE, stride=block), :]
+        return jnp.concatenate([most, tail_ref[pl.ds(j, SPARE, stride=block), :]], axis=0)
+
+    facts = row(words)
+    facts_ref[...] = facts
     across = facts.astype(jnp.float32).T
     id_rows = across[:cap].astype(jnp.int32) - 1
     scale_rows = jnp.exp2(across[cap : 2 * cap]).astype(jnp.bfloat16)
@@ -125,7 +136,7 @@
     items = iota((own, sources), 0).astype(jnp.int16)
     total = jnp.zeros((own, 2 * lanes), jnp.float32)
     for j in range(words):
-        word = message_ref[pl.ds(j, sources, stride=block), :]
+        word = row(j)
         for s, code in ((j, (word << 16) >> 16), (j + words, word >> 16)):
             code = code.astype(jnp.float32)
             value = code * jnp.abs(code)
@@ -137,9 +148,9 @@
     coarse = own // fine
     counts = jnp.zeros((coarse, fine), jnp.float32)
     for s in range(cap):
-        row = id_rows[s : s + 1]
-        whole = (iota((coarse, sources), 0) == lax.div(row, fine)).astype(jnp.bfloat16)
-        rest = (iota((fine, sources), 0) == lax.rem(row, fine)).astype(jnp.bfloat16)
+        ids = id_rows[s : s + 1]
+        whole = (iota((coarse, sources), 0) == lax.div(ids, fine)).astype(jnp.bfloat16)
+        rest = (iota((fine, sources), 0) == lax.rem(ids, fine)).astype(jnp.bfloat16)
         counts = counts + dot_nt(whole, rest)
     counts = jnp.minimum(counts, 1.0).astype(jnp.bfloat16)
     whole = (lax.div(iota((own, coarse), 0), fine) == iota((own, coarse), 1)).astype(jnp.bfloat16)
@@ -169,7 +180,7 @@
     spots = iota((cap * part, half), 1).astype(jnp.int16)
 
     def answer_part(p, carry):
-        ids = message_ref[pl.ds(p * part * block + words, part, stride=block), :] - 1
+        ids = facts_ref[pl.ds(pl.multiple_of(p * part, part), part), :] - 1
         wanted = jnp.concatenate([jnp.broadcast_to(ids[:, s : s + 1], (part, lanes)) for s in range(cap)], axis=0)
         upper = wanted >= half
         spot = jnp.where(upper, wanted - half, wanted).astype(jnp.int16)
@@ -177,9 +188,9 @@
         both = dot(hit, halves_ref[...])
         found = jnp.where(upper, both[:, lanes:], both[:, :lanes])
         for s in range(cap):
-            spread_ref[pl.ds(p * part * cap + s, part, stride=cap), :] = found[s * part : (s + 1) * part]
+            spread_ref[pl.ds(s, part, stride=cap), :] = found[s * part : (s + 1) * part]
         rows = pl.ds(pl.multiple_of(p * part * cap, part * cap), part * cap)
-        answer_ref[rows, :] = spread_ref[rows, :].astype(jnp.bfloat16)
+        answer_ref[rows, :] = spread_ref[: part * cap].astype(jnp.bfloat16)
         return carry
 
     lax.fori_loop(0, 2, answer_part, 0)
@@ -229,7 +240,7 @@
             pltpu.VMEM((1, count), jnp.int32),
             pltpu.VMEM((1, count), jnp.int32),
             pltpu.VMEM((count, width), jnp.float32),
-            pltpu.VMEM((peers * block, lanes), jnp.int32),
+            pltpu.VMEM((peers * block + SPARE, lanes), jnp.int32),
             pltpu.VMEM((count, groups * cap), jnp.bfloat16),
             pltpu.SemaphoreType.DMA((2,)),
             pltpu.SemaphoreType.DMA,
@@ -249,7 +260,9 @@
         in_specs=[VMEM, VMEM, VMEM, VMEM, VMEM],
         out_specs=(HBM, HBM, HBM, VMEM),
         scratch_shapes=[
-            pltpu.VMEM((peers * cap, lanes), jnp.float32),
+            pltpu.VMEM((SPARE * block + SPARE, lanes), jnp.int32),
+            pltpu.VMEM((peers, lanes), jnp.int32),
+            pltpu.VMEM((peers * cap // 2 + SPARE, lanes), jnp.float32),
             pltpu.VMEM((own // 2, 2 * lanes), jnp.bfloat16),
             pltpu.VMEM((3, own, lanes), jnp.float32),
             pltpu.SemaphoreType.DMA((3,)),

time: 116 us -> 116 us (level)
  no operation moved by 1% of the time
where the time goes in v7:
time: 116 us
  blocking collectives  43.1 us (37%)
  waiting for transfers between devices  38.7 us (33%)
  starting transfers between devices  22.2 us (19%)
  Pallas kernels  10.4 us (9%)
  between operations  1.34 us (1%)
    all_to_all x1, blocking collectives, local(): lax.all_to_all(answer, ORDER, split_axis=0, concat_axis=0, tiled=True)  43.1 us
    all_to_all x1, waiting for transfers between devices, local(): lax.all_to_all(message, ORDER, split_axis=0, concat_axis=0, tiled=True)  38.7 us
    all_to_all x1, starting transfers between devices, local(): lax.all_to_all(message, ORDER, split_axis=0, concat_axis=0, tiled=True)  22.2 us
    pallas_call x1, Pallas kernels, local(): pl.pallas_call(functools.partial(update_kernel, cap), out_shape=(table, t...  5.47 us
    pallas_call x1, Pallas kernels, local(): pl.pallas_call(functools.partial(pack_kernel, groups, cap), out_shape=(ja...  3.49 us
  transfers between devices with their start and end apart: 1, of which 1 were waited for; matrix products, arithmetic and copies ran while one was open for 0% of the time, Pallas kernels for 0%

profile of v7, /device:TPU:1, one launch (start us, length us, event | category | flops | bytes accessed | tf_op | source)
XLA Modules:
  0.0 115.7 jit_solution(17864044693721855787)
XLA Ops:
  0.6 3.5 %pack.1 = (s32[2560,128]{1,0:T(8,128)}, bf16[256,512]{1,0:T(8,128)(2,1)}) custom-call(s32[1,256]{1,0:T(1,128)} %bitcast.12, s32[1,256]{1,0:T(1,128)} %bitcast.13, f32[256,1024]{1,0:T(8,128)} %grads_hbm.1), custom_call_target="tpu_custom_call" | custom-call | tf_op jit(solution)/shard_map/pack/pallas_call | solution.py:231
  4.1 0.0 copy-start
  4.1 0.0 copy-start.1
  4.2 0.0 copy-start.2
  4.2 22.2 %all-to-all-start = ((s32[512,1,640]{2,1,0:T(1,128)}), s32[512,1,640]{2,1,0:T(1,128)S(1)}, u32[]{:S(2)}, u32[]{:S(2)}) async-start(s32[512,1,640]{2,1,0:T(1,128)} %bitcast.11), calls=%async_computation | async-start | bytes 2621440 | tf_op jit(solution)/shard_map/all_to_all | solution.py:254
  27.0 38.7 %all-to-all-done = s32[512,1,640]{2,1,0:T(1,128)S(1)} async-done(((s32[512,1,640]{2,1,0:T(1,128)}), s32[512,1,640]{2,1,0:T(1,128)S(1)}, u32[]{:S(2)}, u32[]{:S(2)}) %all-to-all-start) | async-done | bytes 1310752 | tf_op jit(solution)/shard_map/all_to_all | solution.py:254
  65.7 0.0 copy-done
  65.7 0.0 copy-done.1
  65.7 0.0 copy-done.2
  65.7 5.5 %update.1 = (f32[1024,128]{1,0:T(8,128)}, f32[1024,128]{1,0:T(8,128)}, f32[1024,128]{1,0:T(8,128)}, bf16[4096,128]{1,0:T(8,128)(2,1)S(1)}) custom-call(s32[2560,128]{1,0:T(8,128)S(1)} %bitcast.8, s32[1,1]{1,0:T(1,128)} %bitcast.7.step_ref, f32[1024,128]{1,0:T(8,128)S(1)} %copy-done, f32[1024,128]{1,0:T(8,128)S(1)} %copy-done.1, f32[1024,128]{1,0:T(8,128)S(1)} %copy-done.2), custom_call_target="tpu_custom_call" | custom-call | tf_op jit(solution)/shard_map/update/pallas_call | solution.py:257
  71.2 0.0 copy-start.3
  71.2 43.1 %all_to_all.10 = bf16[512,8,128]{2,1,0:T(8,128)(2,1)S(1)} all-to-all(bf16[512,8,128]{2,1,0:T(8,128)(2,1)S(1)} %bitcast.10), channel_id=1, replica_groups=mesh['rows'=64,'cols'=8] {'cols','rows'}, dimensions={0} | all-to-all | bytes 2097152 | tf_op jit(solution)/shard_map/all_to_all | solution.py:274
  114.3 0.0 copy-done.3
  114.3 1.4 %unpack.1 = bf16[256,1024]{1,0:T(8,128)(2,1)} custom-call(bf16[256,512]{1,0:T(8,128)(2,1)S(1)} %copy-done.3, bf16[4096,128]{1,0:T(8,128)(2,1)S(1)} %bitcast.9), custom_call_target="tpu_custom_call" | custom-call | tf_op jit(solution)/shard_map/unpack/pallas_call | solution.py:275
Async XLA Ops:
  4.1 61.6 %copy-start = (f32[1024,128]{1,0:T(8,128)S(1)}, f32[1024,128]{1,0:T(8,128)}, u32[]{:S(2)}) copy-start(f32[1024,128]{1,0:T(8,128)} %params_ref.1) | copy-start | bytes 1572868
  4.1 61.5 %copy-start.1 = (f32[1024,128]{1,0:T(8,128)S(1)}, f32[1024,128]{1,0:T(8,128)}, u32[]{:S(2)}) copy-start(f32[1024,128]{1,0:T(8,128)} %first_ref.1) | copy-start | bytes 1572868
  4.2 61.5 %copy-start.2 = (f32[1024,128]{1,0:T(8,128)S(1)}, f32[1024,128]{1,0:T(8,128)}, u32[]{:S(2)}) copy-start(f32[1024,128]{1,0:T(8,128)} %second_ref.1) | copy-start | bytes 1572868
  4.2 61.5 %all-to-all-start = ((s32[512,1,640]{2,1,0:T(1,128)}), s32[512,1,640]{2,1,0:T(1,128)S(1)}, u32[]{:S(2)}, u32[]{:S(2)}) async-start(s32[512,1,640]{2,1,0:T(1,128)} %bitcast.11), calls=%async_computation | async-start | bytes 2621440 | tf_op jit(solution)/shard_map/all_to_all | solution.py:254
  71.2 43.1 %copy-start.3 = (bf16[256,512]{1,0:T(8,128)(2,1)S(1)}, bf16[256,512]{1,0:T(8,128)(2,1)}, u32[]{:S(2)}) copy-start(bf16[256,512]{1,0:T(8,128)(2,1)} %get-tuple-element.14.select_ref) | copy-start | bytes 786436

commit v8 on v7

--- a/solution.py
+++ b/solution.py
@@ -73,6 +73,14 @@
     stores = [pltpu.make_async_copy(select_ref, select_hbm, select_sem)]
     stores[0].start()
 
+    named = ids_ref[...] + 1
+    lane = iota((LANES, count), 0)
+    at_id = lane == position
+    at_power = lane == position + cap
+    names_high = jnp.where(at_id, lax.div(named, 32).astype(jnp.float32), 0.0).astype(jnp.bfloat16)
+    names_low = jnp.where(at_id, lax.rem(named, 32).astype(jnp.float32), 0.0).astype(jnp.bfloat16)
+    facts = dot_nt(mine_half, names_high) * 32.0 + dot_nt(mine_half, names_low)
+
     load.wait()
     grads = grads_ref[...]
     size = jnp.abs(grads)
@@ -85,14 +93,8 @@
     high = high.astype(jnp.bfloat16)
 
     power_row = jnp.sum(jnp.where(on_diagonal, power, 0.0), axis=0, keepdims=True)
-    named = ids_ref[...] + 1
-    lane = iota((LANES, count), 0)
-    at_id = lane == position
-    at_power = lane == position + cap
-    facts_high = jnp.where(at_id, lax.div(named, 32).astype(jnp.float32), 0.0).astype(jnp.bfloat16)
-    facts_low = jnp.where(at_id, lax.rem(named, 32).astype(jnp.float32), jnp.where(at_power, power_row, 0.0))
-    facts = dot_nt(mine_half, facts_high) * 32.0 + dot_nt(mine_half, facts_low.astype(jnp.bfloat16))
-    facts = facts.astype(jnp.int32)
+    powers = jnp.where(at_power, power_row, 0.0).astype(jnp.bfloat16)
+    facts = (facts + dot_nt(mine_half, powers)).astype(jnp.int32)
 
     for c in range(slices):
         columns = slice(c * LANES, (c + 1) * LANES)
@@ -133,17 +135,6 @@
     id_rows = across[:cap].astype(jnp.int32) - 1
     scale_rows = jnp.exp2(across[cap : 2 * cap]).astype(jnp.bfloat16)
     short_rows = id_rows.astype(jnp.int16)
-    items = iota((own, sources), 0).astype(jnp.int16)
-    total = jnp.zeros((own, 2 * lanes), jnp.float32)
-    for j in range(words):
-        word = row(j)
-        for s, code in ((j, (word << 16) >> 16), (j + words, word >> 16)):
-            code = code.astype(jnp.float32)
-            value = code * jnp.abs(code)
-            high = value.astype(jnp.bfloat16)
-            low = (value - high.astype(jnp.float32)).astype(jnp.bfloat16)
-            hit = jnp.where(items == short_rows[s : s + 1], scale_rows[s : s + 1], jnp.bfloat16(0))
-            total = total + dot(hit, jnp.concatenate([high, low], axis=1))
     fine = 32
     coarse = own // fine
     counts = jnp.zeros((coarse, fine), jnp.float32)
@@ -156,6 +147,17 @@
     whole = (lax.div(iota((own, coarse), 0), fine) == iota((own, coarse), 1)).astype(jnp.bfloat16)
     rest = lax.rem(iota((own, fine), 0), fine) == iota((own, fine), 1)
     live = jnp.sum(jnp.where(rest, dot(whole, counts), 0.0), axis=1, keepdims=True) > 0.0
+    items = iota((own, sources), 0).astype(jnp.int16)
+    total = jnp.zeros((own, 2 * lanes), jnp.float32)
+    for j in range(words):
+        word = row(j)
+        for s, code in ((j, (word << 16) >> 16), (j + words, word >> 16)):
+            code = code.astype(jnp.float32)
+            value = code * jnp.abs(code)
+            high = value.astype(jnp.bfloat16)
+            low = (value - high.astype(jnp.float32)).astype(jnp.bfloat16)
+            hit = jnp.where(items == short_rows[s : s + 1], scale_rows[s : s + 1], jnp.bfloat16(0))
+            total = total + dot(hit, jnp.concatenate([high, low], axis=1))
     summed = (total[:, :lanes] + total[:, lanes:]) * (1.0 / (FULL * FULL))
     fix_first = one_minus_power(0.9, step_ref[...])
     fix_second = one_minus_power(0.999, step_ref[...])
@@ -202,11 +204,11 @@
     select = select_ref[...]
     slots = select.shape[1]
     copies = []
-    for c in range(out_ref.shape[1] // LANES):
-        columns = pl.ds(c * LANES, LANES)
-        rows = dot(select, back_ref[c * slots : (c + 1) * slots])
-        out_ref[:, columns] = rows.astype(jnp.bfloat16)
-        copies.append(pltpu.make_async_copy(out_ref.at[:, columns], out_hbm.at[:, columns], out_sem.at[c]))
+    for c in range(0, out_ref.shape[1] // LANES, 2):
+        columns = pl.ds(c * LANES, 2 * LANES)
+        one, two = back_ref[c * slots : (c + 1) * slots], back_ref[(c + 1) * slots : (c + 2) * slots]
+        out_ref[:, columns] = dot(select, jnp.concatenate([one, two], axis=1)).astype(jnp.bfloat16)
+        copies.append(pltpu.make_async_copy(out_ref.at[:, columns], out_hbm.at[:, columns], out_sem.at[c // 2]))
         copies[-1].start()
     for copy in copies:
         copy.wait()
@@ -277,7 +279,7 @@
         out_shape=jax.ShapeDtypeStruct((count, width), jnp.bfloat16),
         in_specs=[VMEM, VMEM],
         out_specs=HBM,
-        scratch_shapes=[pltpu.VMEM((count, width), jnp.bfloat16), pltpu.SemaphoreType.DMA((slices,))],
+        scratch_shapes=[pltpu.VMEM((count, width), jnp.bfloat16), pltpu.SemaphoreType.DMA((slices // 2,))],
         compiler_params=params_for(40),
         name="unpack",
     )(select, answer.reshape(peers * cap, lanes))

time: 116 us -> 116 us (level)
  no operation moved by 1% of the time
where the time goes in v8:
time: 116 us; the launch traced here: 115 us
  blocking collectives  43.2 us (37%)
  waiting for transfers between devices  38.7 us (33%)
  starting transfers between devices  22.2 us (19%)
  Pallas kernels  10 us (9%)
  between operations  1.34 us (1%)
    all_to_all x1, blocking collectives, local(): lax.all_to_all(answer, ORDER, split_axis=0, concat_axis=0, tiled=True)  43.2 us
    all_to_all x1, waiting for transfers between devices, local(): lax.all_to_all(message, ORDER, split_axis=0, concat_axis=0, tiled=True)  38.7 us
    all_to_all x1, starting transfers between devices, local(): lax.all_to_all(message, ORDER, split_axis=0, concat_axis=0, tiled=True)  22.2 us
    pallas_call x1, Pallas kernels, local(): pl.pallas_call(functools.partial(update_kernel, cap), out_shape=(table, t...  5.4 us
    pallas_call x1, Pallas kernels, local(): pl.pallas_call(functools.partial(pack_kernel, groups, cap), out_shape=(ja...  3.46 us
  transfers between devices with their start and end apart: 1, of which 1 were waited for; matrix products, arithmetic and copies ran while one was open for 0% of the time, Pallas kernels for 0%

profile of v8, /device:TPU:1, one launch (start us, length us, event | category | flops | bytes accessed | tf_op | source)
XLA Modules:
  0.0 115.4 jit_solution(17261241465513962026)
XLA Ops:
  0.6 3.5 %pack.1 = (s32[2560,128]{1,0:T(8,128)}, bf16[256,512]{1,0:T(8,128)(2,1)}) custom-call(s32[1,256]{1,0:T(1,128)} %bitcast.12, s32[1,256]{1,0:T(1,128)} %bitcast.13, f32[256,1024]{1,0:T(8,128)} %grads_hbm.1), custom_call_target="tpu_custom_call" | custom-call | tf_op jit(solution)/shard_map/pack/pallas_call | solution.py:233
  4.1 0.0 copy-start
  4.1 0.0 copy-start.1
  4.1 0.0 copy-start.2
  4.1 22.2 %all-to-all-start = ((s32[512,1,640]{2,1,0:T(1,128)}), s32[512,1,640]{2,1,0:T(1,128)S(1)}, u32[]{:S(2)}, u32[]{:S(2)}) async-start(s32[512,1,640]{2,1,0:T(1,128)} %bitcast.11), calls=%async_computation | async-start | bytes 2621440 | tf_op jit(solution)/shard_map/all_to_all | solution.py:256
  27.0 38.7 %all-to-all-done = s32[512,1,640]{2,1,0:T(1,128)S(1)} async-done(((s32[512,1,640]{2,1,0:T(1,128)}), s32[512,1,640]{2,1,0:T(1,128)S(1)}, u32[]{:S(2)}, u32[]{:S(2)}) %all-to-all-start) | async-done | bytes 1310752 | tf_op jit(solution)/shard_map/all_to_all | solution.py:256
  65.7 0.0 copy-done
  65.7 0.0 copy-done.1
  65.7 0.0 copy-done.2
  65.7 5.4 %update.1 = (f32[1024,128]{1,0:T(8,128)}, f32[1024,128]{1,0:T(8,128)}, f32[1024,128]{1,0:T(8,128)}, bf16[4096,128]{1,0:T(8,128)(2,1)S(1)}) custom-call(s32[2560,128]{1,0:T(8,128)S(1)} %bitcast.8, s32[1,1]{1,0:T(1,128)} %bitcast.7.step_ref, f32[1024,128]{1,0:T(8,128)S(1)} %copy-done, f32[1024,128]{1,0:T(8,128)S(1)} %copy-done.1, f32[1024,128]{1,0:T(8,128)S(1)} %copy-done.2), custom_call_target="tpu_custom_call" | custom-call | tf_op jit(solution)/shard_map/update/pallas_call | solution.py:259
  71.1 0.0 copy-start.3
  71.1 43.2 %all_to_all.10 = bf16[512,8,128]{2,1,0:T(8,128)(2,1)S(1)} all-to-all(bf16[512,8,128]{2,1,0:T(8,128)(2,1)S(1)} %bitcast.10), channel_id=1, replica_groups=mesh['rows'=64,'cols'=8] {'cols','rows'}, dimensions={0} | all-to-all | bytes 2097152 | tf_op jit(solution)/shard_map/all_to_all | solution.py:276
  114.2 0.0 copy-done.3
  114.2 1.2 %unpack.1 = bf16[256,1024]{1,0:T(8,128)(2,1)} custom-call(bf16[256,512]{1,0:T(8,128)(2,1)S(1)} %copy-done.3, bf16[4096,128]{1,0:T(8,128)(2,1)S(1)} %bitcast.9), custom_call_target="tpu_custom_call" | custom-call | tf_op jit(solution)/shard_map/unpack/pallas_call | solution.py:277
Async XLA Ops:
  4.1 61.6 %copy-start = (f32[1024,128]{1,0:T(8,128)S(1)}, f32[1024,128]{1,0:T(8,128)}, u32[]{:S(2)}) copy-start(f32[1024,128]{1,0:T(8,128)} %params_ref.1) | copy-start | bytes 1572868
  4.1 61.5 %copy-start.1 = (f32[1024,128]{1,0:T(8,128)S(1)}, f32[1024,128]{1,0:T(8,128)}, u32[]{:S(2)}) copy-start(f32[1024,128]{1,0:T(8,128)} %first_ref.1) | copy-start | bytes 1572868
  4.1 61.5 %copy-start.2 = (f32[1024,128]{1,0:T(8,128)S(1)}, f32[1024,128]{1,0:T(8,128)}, u32[]{:S(2)}) copy-start(f32[1024,128]{1,0:T(8,128)} %second_ref.1) | copy-start | bytes 1572868
  4.1 61.5 %all-to-all-start = ((s32[512,1,640]{2,1,0:T(1,128)}), s32[512,1,640]{2,1,0:T(1,128)S(1)}, u32[]{:S(2)}, u32[]{:S(2)}) async-start(s32[512,1,640]{2,1,0:T(1,128)} %bitcast.11), calls=%async_computation | async-start | bytes 2621440 | tf_op jit(solution)/shard_map/all_to_all | solution.py:256
  71.1 43.2 %copy-start.3 = (bf16[256,512]{1,0:T(8,128)(2,1)S(1)}, bf16[256,512]{1,0:T(8,128)(2,1)}, u32[]{:S(2)}) copy-start(bf16[256,512]{1,0:T(8,128)(2,1)} %get-tuple-element.14.select_ref) | copy-start | bytes 786436

commit v9 on v8

--- a/solution.py
+++ b/solution.py
@@ -164,7 +164,7 @@
     first, second, params = first_ref[...], second_ref[...], params_ref[...]
     new_first = jnp.where(live, 0.9 * first + 0.1 * summed, first)
     new_second = jnp.where(live, 0.999 * second + 0.001 * summed * summed, second)
-    direction = -(new_first / fix_first) / (jnp.sqrt(new_second / fix_second) + 1e-08)
+    direction = -(new_first * (1.0 / fix_first)) / (jnp.sqrt(new_second * (1.0 / fix_second)) + 1e-08)
     table_ref[0] = jnp.where(live, params + 0.01 * direction, params)
     table_ref[1] = new_first
     table_ref[2] = new_second
@@ -186,7 +186,7 @@
         wanted = jnp.concatenate([jnp.broadcast_to(ids[:, s : s + 1], (part, lanes)) for s in range(cap)], axis=0)
         upper = wanted >= half
         spot = jnp.where(upper, wanted - half, wanted).astype(jnp.int16)
-        hit = (spots == jnp.concatenate([spot] * (half // lanes), axis=1)).astype(jnp.bfloat16)
+        hit = jnp.where(spots == jnp.concatenate([spot] * (half // lanes), axis=1), jnp.bfloat16(1), jnp.bfloat16(0))
         both = dot(hit, halves_ref[...])
         found = jnp.where(upper, both[:, lanes:], both[:, :lanes])
         for s in range(cap):

time: 116 us -> 115 us (level)
  no operation moved by 1% of the time
where the time goes in v9:
time: 115 us
  blocking collectives  43.2 us (38%)
  waiting for transfers between devices  38.7 us (34%)
  starting transfers between devices  22.2 us (19%)
  Pallas kernels  9.4 us (8%)
  between operations  1.34 us (1%)
    all_to_all x1, blocking collectives, local(): lax.all_to_all(answer, ORDER, split_axis=0, concat_axis=0, tiled=True)  43.2 us
    all_to_all x1, waiting for transfers between devices, local(): lax.all_to_all(message, ORDER, split_axis=0, concat_axis=0, tiled=True)  38.7 us
    all_to_all x1, starting transfers between devices, local(): lax.all_to_all(message, ORDER, split_axis=0, concat_axis=0, tiled=True)  22.2 us
    pallas_call x1, Pallas kernels, local(): pl.pallas_call(functools.partial(update_kernel, cap), out_shape=(table, t...  4.76 us
    pallas_call x1, Pallas kernels, local(): pl.pallas_call(functools.partial(pack_kernel, groups, cap), out_shape=(ja...  3.46 us
  transfers between devices with their start and end apart: 1, of which 1 were waited for; matrix products, arithmetic and copies ran while one was open for 0% of the time, Pallas kernels for 0%

profile of v9, /device:TPU:1, one launch (start us, length us, event | category | flops | bytes accessed | tf_op | source)
XLA Modules:
  0.0 114.8 jit_solution(17833166839678692840)
XLA Ops:
  0.6 3.5 %pack.1 = (s32[2560,128]{1,0:T(8,128)}, bf16[256,512]{1,0:T(8,128)(2,1)}) custom-call(s32[1,256]{1,0:T(1,128)} %bitcast.12, s32[1,256]{1,0:T(1,128)} %bitcast.13, f32[256,1024]{1,0:T(8,128)} %grads_hbm.1), custom_call_target="tpu_custom_call" | custom-call | tf_op jit(solution)/shard_map/pack/pallas_call | solution.py:233
  4.1 0.0 copy-start
  4.1 0.0 copy-start.1
  4.1 0.0 copy-start.2
  4.1 22.2 %all-to-all-start = ((s32[512,1,640]{2,1,0:T(1,128)}), s32[512,1,640]{2,1,0:T(1,128)S(1)}, u32[]{:S(2)}, u32[]{:S(2)}) async-start(s32[512,1,640]{2,1,0:T(1,128)} %bitcast.11), calls=%async_computation | async-start | bytes 2621440 | tf_op jit(solution)/shard_map/all_to_all | solution.py:256
  27.0 38.7 %all-to-all-done = s32[512,1,640]{2,1,0:T(1,128)S(1)} async-done(((s32[512,1,640]{2,1,0:T(1,128)}), s32[512,1,640]{2,1,0:T(1,128)S(1)}, u32[]{:S(2)}, u32[]{:S(2)}) %all-to-all-start) | async-done | bytes 1310752 | tf_op jit(solution)/shard_map/all_to_all | solution.py:256
  65.7 0.0 copy-done
  65.7 0.0 copy-done.1
  65.7 0.0 copy-done.2
  65.7 4.8 %update.1 = (f32[1024,128]{1,0:T(8,128)}, f32[1024,128]{1,0:T(8,128)}, f32[1024,128]{1,0:T(8,128)}, bf16[4096,128]{1,0:T(8,128)(2,1)S(1)}) custom-call(s32[2560,128]{1,0:T(8,128)S(1)} %bitcast.8, s32[1,1]{1,0:T(1,128)} %bitcast.7.step_ref, f32[1024,128]{1,0:T(8,128)S(1)} %copy-done, f32[1024,128]{1,0:T(8,128)S(1)} %copy-done.1, f32[1024,128]{1,0:T(8,128)S(1)} %copy-done.2), custom_call_target="tpu_custom_call" | custom-call | tf_op jit(solution)/shard_map/update/pallas_call | solution.py:259
  70.4 0.0 copy-start.3
  70.4 43.2 %all_to_all.10 = bf16[512,8,128]{2,1,0:T(8,128)(2,1)S(1)} all-to-all(bf16[512,8,128]{2,1,0:T(8,128)(2,1)S(1)} %bitcast.10), channel_id=1, replica_groups=mesh['rows'=64,'cols'=8] {'cols','rows'}, dimensions={0} | all-to-all | bytes 2097152 | tf_op jit(solution)/shard_map/all_to_all | solution.py:276
  113.6 0.0 copy-done.3
  113.6 1.2 %unpack.1 = bf16[256,1024]{1,0:T(8,128)(2,1)} custom-call(bf16[256,512]{1,0:T(8,128)(2,1)S(1)} %copy-done.3, bf16[4096,128]{1,0:T(8,128)(2,1)S(1)} %bitcast.9), custom_call_target="tpu_custom_call" | custom-call | tf_op jit(solution)/shard_map/unpack/pallas_call | solution.py:277
Async XLA Ops:
  4.1 61.6 %copy-start = (f32[1024,128]{1,0:T(8,128)S(1)}, f32[1024,128]{1,0:T(8,128)}, u32[]{:S(2)}) copy-start(f32[1024,128]{1,0:T(8,128)} %params_ref.1) | copy-start | bytes 1572868
  4.1 61.5 %copy-start.1 = (f32[1024,128]{1,0:T(8,128)S(1)}, f32[1024,128]{1,0:T(8,128)}, u32[]{:S(2)}) copy-start(f32[1024,128]{1,0:T(8,128)} %first_ref.1) | copy-start | bytes 1572868
  4.1 61.5 %copy-start.2 = (f32[1024,128]{1,0:T(8,128)S(1)}, f32[1024,128]{1,0:T(8,128)}, u32[]{:S(2)}) copy-start(f32[1024,128]{1,0:T(8,128)} %second_ref.1) | copy-start | bytes 1572868
  4.1 61.5 %all-to-all-start = ((s32[512,1,640]{2,1,0:T(1,128)}), s32[512,1,640]{2,1,0:T(1,128)S(1)}, u32[]{:S(2)}, u32[]{:S(2)}) async-start(s32[512,1,640]{2,1,0:T(1,128)} %bitcast.11), calls=%async_computation | async-start | bytes 2621440 | tf_op jit(solution)/shard_map/all_to_all | solution.py:256
  70.4 43.2 %copy-start.3 = (bf16[256,512]{1,0:T(8,128)(2,1)S(1)}, bf16[256,512]{1,0:T(8,128)(2,1)}, u32[]{:S(2)}) copy-start(bf16[256,512]{1,0:T(8,128)(2,1)} %get-tuple-element.14.select_ref) | copy-start | bytes 786436
